TPU v7x, 256 devices: a whole 4x4x8 slice. The times are simulated.
256 devices in a mesh: graph: 64 (over x, z, core), slab: 4 (over y).
Axes of the slice: x: 4, y: 4, z: 8, core: 2. Of those that a mesh axis runs over, the one named last changes fastest.
Arguments:
- feats: bfloat16 [64, 4, 256, 256], P('graph', 'slab'), may hold values from -6 to 6
- w_self: bfloat16 [256, 256], replicated, may hold values from -0.375 to 0.375
- w_neigh: bfloat16 [256, 256], replicated, may hold values from -0.375 to 0.375
- block_vals: bfloat16 [64, 4, 32, 128, 128], P('graph', 'slab'), may hold values from -0.125 to 0.125
- block_dst: int32 [64, 4, 32], P('graph', 'slab'), may hold values from 0 to 1
- block_src: int32 [64, 4, 32], P('graph', 'slab'), may hold values from 0 to 7
- block_count: int32 [64, 4], P('graph', 'slab'), may hold values from 8 to 32, as said below
- prev_partial: bfloat16 [64, 4, 256, 256], P('graph', 'slab'), may hold values from -6 to 6
- mirror_rows: int32 [64, 4, 64, 4], P('graph', 'slab'), may hold values from 0 to 255, as said below
- send_count: int32 [64, 4, 64], P('graph', 'slab'), may hold values from 0 to 4, as said below
- master_rows: int32 [64, 4, 64, 4], P('graph', 'slab'), may hold values from 0 to 255
- momentum: float32 [64, 4, 256, 256], P('graph', 'slab'), may hold values from -6 to 6
- cotangent: bfloat16 [64, 4, 256, 256], P('graph', 'slab'), may hold values from -6 to 6
- prev_grad: bfloat16 [64, 4, 256, 256], P('graph', 'slab'), may hold values from -6 to 6
- grad_momentum: float32 [64, 4, 256, 256], P('graph', 'slab'), may hold values from -6 to 6
Outputs:
- hidden: bfloat16 [64, 4, 256, 256], P('graph', 'slab')
- feat_grad: bfloat16 [64, 4, 256, 256], P('graph', 'slab')
- smoothed_partials: float32 [64, 4, 256, 256], P('graph', 'slab')
- smoothed_grads: float32 [64, 4, 256, 256], P('graph', 'slab')
- w_grads: float32 [2, 256, 256], replicated
Inputs may be any that keep to these rules, and one draw needn't show every extreme that they name: `block_count`: blocks at positions at or past the count are ignored; some device has all 32 live in every draw. `mirror_rows`: rows are distinct over all peers and slots of one device. `send_count`: slots at or past the count are ignored; a device's count for its own partition is 0; every device has 4 for some peer.
All inputs are finite; a program needn't handle non-finite values.
Results may differ from a plain program's by a relative error of at most 0.022.
The roundings to bfloat16 on the way count: a program that leaves them out, or rounds other values in their place, can miss the bound.
Values may be sent and summed in bfloat16 or wider, within the bound.
A program may use at most 64 MiB of HBM per device.

v0:
```python
import jax
import jax.numpy as jnp
from jax import lax
from jax.sharding import PartitionSpec as P

SMOOTHING = 0.7


def tile_products(vals, pick_index, sum_index, count, tiles, n_sum, flipped):
    form = "bji,bjf->bif" if flipped else "bij,bjf->bif"
    blocks = vals.shape[0]
    chosen = tiles[pick_index]
    prods = jnp.einsum(form, vals, chosen, preferred_element_type=jnp.float32)
    live = jnp.arange(blocks, dtype=jnp.int32) < count
    prods = jnp.where(live[:, None, None], prods, 0.0)
    return jax.ops.segment_sum(prods, sum_index, num_segments=n_sum)


def add_rows(values, rows, total_rows):
    width = values.shape[-1]
    start = jnp.zeros((total_rows, width), jnp.float32)
    return start.at[rows.reshape(-1)].add(values.reshape(-1, width).astype(jnp.float32))


def shards(
    feats,
    w_self,
    w_neigh,
    block_vals,
    block_dst,
    block_src,
    block_count,
    prev_partial,
    mirror_rows,
    send_count,
    master_rows,
    momentum,
    cotangent,
    prev_grad,
    grad_momentum,
):
    own = feats[0, 0]
    rows_dev = own.shape[0]
    width = own.shape[1]
    vals = block_vals[0, 0]
    size = vals.shape[1]
    dst = block_dst[0, 0]
    src = block_src[0, 0]
    count = block_count[0, 0]
    mirrors = mirror_rows[0, 0]
    masters = master_rows[0, 0]
    slots = mirrors.shape[1]
    slabs = lax.axis_size("slab")
    live_slot = jnp.arange(slots, dtype=jnp.int32)[None, :] < send_count[0, 0][:, None]
    outgoing = jnp.where(
        live_slot[..., None], prev_partial[0, 0][mirrors], jnp.zeros((), jnp.bfloat16)
    )
    back_out = prev_grad[0, 0][masters]
    arrived = lax.all_to_all(outgoing, "graph", split_axis=0, concat_axis=0, tiled=True)
    boundary = add_rows(arrived, masters, rows_dev)
    smoothed_partials = SMOOTHING * momentum[0, 0] + (1.0 - SMOOTHING) * boundary
    group = lax.all_gather(own, "slab", axis=0, tiled=True)
    group_tiles = group.reshape(slabs * rows_dev // size, size, width)
    local = tile_products(vals, src, dst, count, group_tiles, rows_dev // size, False).reshape(
        rows_dev, width
    )
    agg = (local + smoothed_partials).astype(jnp.bfloat16)
    pre = jnp.dot(own, w_self, preferred_element_type=jnp.float32) + jnp.dot(
        agg, w_neigh, preferred_element_type=jnp.float32
    )
    hidden = jnp.maximum(pre, 0.0).astype(jnp.bfloat16)
    grad_in = cotangent[0, 0]
    delta = jnp.where(pre > 0, grad_in, jnp.zeros_like(grad_in))
    grad_self = jnp.dot(own.T, delta, preferred_element_type=jnp.float32)
    grad_neigh = jnp.dot(agg.T, delta, preferred_element_type=jnp.float32)
    summed = lax.psum(jnp.stack([grad_self, grad_neigh]), ("graph", "slab"))
    total_rows = lax.axis_size("graph") * slabs * rows_dev
    w_grads = summed * (1.0 / jnp.sqrt(jnp.float32(total_rows)))
    back_in = lax.all_to_all(back_out, "graph", split_axis=0, concat_axis=0, tiled=True)
    back_in = jnp.where(live_slot[..., None], back_in, jnp.zeros((), jnp.bfloat16))
    returned = add_rows(back_in, mirrors, rows_dev)
    smoothed_grads = SMOOTHING * grad_momentum[0, 0] + (1.0 - SMOOTHING) * returned
    grad_agg = (
        jnp.dot(delta, w_neigh.T, preferred_element_type=jnp.float32) + smoothed_grads
    ).astype(jnp.bfloat16)
    grad_tiles = grad_agg.reshape(rows_dev // size, size, width)
    source_part = tile_products(
        vals, dst, src, count, grad_tiles, slabs * rows_dev // size, True
    ).reshape(slabs * rows_dev, width)
    mine = lax.psum_scatter(source_part, "slab", scatter_dimension=0, tiled=True)
    feat_grad = (jnp.dot(delta, w_self.T, preferred_element_type=jnp.float32) + mine).astype(
        jnp.bfloat16
    )
    return (
        hidden[None, None],
        feat_grad[None, None],
        smoothed_partials[None, None],
        smoothed_grads[None, None],
        w_grads,
    )


def solution(mesh):
    in_specs = (
        P("graph", "slab", None, None),
        P(),
        P(),
        P("graph", "slab", None, None, None),
        P("graph", "slab", None),
        P("graph", "slab", None),
        P("graph", "slab"),
        P("graph", "slab", None, None),
        P("graph", "slab", None, None),
        P("graph", "slab", None),
        P("graph", "slab", None, None),
        P("graph", "slab", None, None),
        P("graph", "slab", None, None),
        P("graph", "slab", None, None),
        P("graph", "slab", None, None),
    )
    out_specs = (
        P("graph", "slab", None, None),
        P("graph", "slab", None, None),
        P("graph", "slab", None, None),
        P("graph", "slab", None, None),
        P(),
    )
    return jax.shard_map(shards, mesh=mesh, in_specs=in_specs, out_specs=out_specs, check_vma=False)
```

profile of v0, /device:TPU:1, one launch (start us, length us, event | category | flops | bytes accessed | tf_op | source)
XLA Modules:
  0.0 345.7 jit_solution(3159560332219177227)
XLA Ops:
  8.0 0.8 compare_select_fusion.3
  8.8 0.1 copy.29
  8.9 0.1 reshape.252
  9.0 1.9 gather_fusion.2
  10.9 0.7 reshape.251
  11.6 13.0 %all-to-all-start.1 = ((bf16[64,4,256]{2,1,0:T(4,128)(2,1)}), bf16[64,4,256]{2,1,0:T(4,128)(2,1)S(1)}, u32[]{:S(2)}, u32[]{:S(2)}) async-start(bf16[64,4,256]{2,1,0:T(4,128)(2,1)} %reshape.251), calls=%async_computation.1 | async-start | bytes 262144 | tf_op jit(solution)/shard_map/all_to_all | solution.py:79
  24.6 0.8 copy.26
  25.4 0.7 compare_select_fusion.4
  26.0 0.8 copy.28
  27.5 11.5 %all-gather = bf16[1,1,1024,256]{3,2,1,0:T(8,128)(2,1)S(1)} all-gather(bf16[1,1,256,256]{3,2,1,0:T(8,128)(2,1)} %param.15), channel_id=2, replica_groups=mesh['graph'=64,'slab'=4] {'slab'}, dimensions={2}, use_global_device_ids=true | all-gather | bytes 655360 | tf_op jit(solution)/shard_map/all_gather | solution.py:62
  39.0 0.7 fusion.16
  39.7 0.1 copy.27
  39.8 0.1 reshape.244
  39.9 0.1 reshape_squeeze.6
  40.0 0.1 reshape_squeeze.7
  40.1 0.7 fusion.17
  40.8 2.0 gather_fusion
  42.8 4.5 %select_bitcast_fusion.1 = f32[32,128,256]{1,2,0:T(8,128)} fusion(bf16[32,128,256]{2,1,0:T(8,128)(2,1)} %gather_fusion, pred[32]{0:T(512)(128)(4,1)S(1)} %iota_compare_fusion.1, bf16[1,1,32,128,128]{4,3,2,1,0:T(8,128)(2,1)S(1)} %copy-done), kind=kOutput, calls=%fused_computation.9 | convolution fusion | flops 269484032 | bytes 7340064 | tf_op jit(solution)/shard_map/bij,bjf->bif/dot_general | solution.py:13
  47.3 1.2 gather_fusion.1
  48.5 0.1 iota_compare_fusion
  48.6 0.9 select_convert_fusion
  49.5 12.3 %all-to-all-start = ((bf16[64,4,256]{2,1,0:T(4,128)(2,1)}), bf16[64,4,256]{2,1,0:T(4,128)(2,1)S(1)}, u32[]{:S(2)}, u32[]{:S(2)}) async-start(bf16[64,4,256]{2,1,0:T(4,128)(2,1)} %get-tuple-element.20), calls=%async_computation | async-start | bytes 262144 | tf_op jit(solution)/shard_map/all_to_all | solution.py:59
  61.8 0.0 all-reduce.2.cloned.1.call-start
  61.9 5.6 %copy.25 = f32[32,128,256]{2,1,0:T(8,128)} copy(f32[32,128,256]{1,2,0:T(8,128)} %select_bitcast_fusion.1) | data formatting | bytes 8388608 | tf_op jit(solution)/shard_map/jit(_where)/select_n | solution.py:15
  67.6 6.4 %scatter_fusion = f32[2,128,256]{2,1,0:T(8,128)S(1)} fusion(f32[2,128,256]{2,1,0:T(8,128)S(1)} %broadcast_in_dim.64, s32[32]{0:T(128)S(1)} %bitcast.97, f32[32,128,256]{2,1,0:T(8,128)} %copy.25), kind=kCustom, calls=%fused_computation.4 | custom fusion | flops 1048576 | bytes 12583040 | tf_op jit(solution)/shard_map/scatter-add | solution.py:16
  74.0 0.2 fusion.8
  74.2 0.1 reshape.286
  74.3 2.0 scatter_custom_fusion.2
  76.4 2.0 scatter_custom_fusion.1
  78.4 0.8 fusion.14
  79.2 1.8 compare_select_fusion
  80.9 0.2 convolution_bitcast_fusion
  81.2 0.2 convolution_bitcast_fusion.1
  81.4 0.8 pad_maximum_fusion
  82.2 0.2 reduce-scatter.2.cloned.1.call-start
  82.5 0.2 fusion.1
  82.7 0.7 gather_fusion.3
  83.4 2.9 select_bitcast_fusion
  86.3 5.6 %copy.31 = f32[32,128,256]{2,1,0:T(8,128)} copy(f32[32,128,256]{1,2,0:T(8,128)} %select_bitcast_fusion) | data formatting | bytes 8388608 | tf_op jit(solution)/shard_map/jit(_where)/select_n | solution.py:15
  92.0 0.1 broadcast_in_dim.71
  92.1 6.5 %scatter_fusion.1 = f32[8,128,256]{2,1,0:T(8,128)S(1)} fusion(f32[8,128,256]{2,1,0:T(8,128)S(1)} %broadcast_in_dim.71, s32[32]{0:T(128)S(1)} %bitcast.98, f32[32,128,256]{2,1,0:T(8,128)} %copy.31), kind=kCustom, calls=%fused_computation.7 | custom fusion | flops 1048576 | bytes 12583040 | tf_op jit(solution)/shard_map/scatter-add | solution.py:16
  98.6 1.0 copy-done.1
  99.5 0.0 reduce-scatter.2.cloned.1.call-update
  99.6 0.7 fusion.15
  100.3 234.1 %all-reduce.2.cloned.1.call-done = f32[2,256,256]{1,2,0:T(8,128)} async-done(((f32[2,256,256]{1,2,0:T(8,128)}), f32[2,256,256]{1,2,0:T(8,128)}) %all-reduce.2.cloned.1.call-update) | async-done | bytes 524304 | tf_op jit(solution)/shard_map/psum | solution.py:76
  334.4 1.1 broadcast_multiply_fusion
  335.5 1.0 copy.33
  336.5 1.8 fusion.2
  (41 shorter events, 0.2 us)
Async XLA Ops:
  8.0 34.8 %copy-start = (bf16[1,1,32,128,128]{4,3,2,1,0:T(8,128)(2,1)S(1)}, bf16[1,1,32,128,128]{4,3,2,1,0:T(8,128)(2,1)}, u32[]{:S(2)}) copy-start(bf16[1,1,32,128,128]{4,3,2,1,0:T(8,128)(2,1)} %param.18) | copy-start | bytes 3145732
  11.6 37.0 %all-to-all-start.1 = ((bf16[64,4,256]{2,1,0:T(4,128)(2,1)}), bf16[64,4,256]{2,1,0:T(4,128)(2,1)S(1)}, u32[]{:S(2)}, u32[]{:S(2)}) async-start(bf16[64,4,256]{2,1,0:T(4,128)(2,1)} %reshape.251), calls=%async_computation.1 | async-start | bytes 262144 | tf_op jit(solution)/shard_map/all_to_all | solution.py:79
  42.8 4.5 %copy-start.2 = (bf16[1,1,256,256]{3,2,1,0:T(8,128)(2,1)S(1)}, bf16[1,1,256,256]{3,2,1,0:T(8,128)(2,1)}, u32[]{:S(2)}) copy-start(bf16[1,1,256,256]{3,2,1,0:T(8,128)(2,1)} %param.22) | copy-start | bytes 393220
  42.8 5.7 %copy-start.13 = (s32[1,1,64]{2,1,0:T(1,128)S(1)}, s32[1,1,64]{2,1,0:T(1,128)}, u32[]{:S(2)}) copy-start(s32[1,1,64]{2,1,0:T(1,128)} %param.24) | copy-start | bytes 772
  49.5 26.9 %all-to-all-start = ((bf16[64,4,256]{2,1,0:T(4,128)(2,1)}), bf16[64,4,256]{2,1,0:T(4,128)(2,1)S(1)}, u32[]{:S(2)}, u32[]{:S(2)}) async-start(bf16[64,4,256]{2,1,0:T(4,128)(2,1)} %get-tuple-element.20), calls=%async_computation | async-start | bytes 262144 | tf_op jit(solution)/shard_map/all_to_all | solution.py:59
  61.8 272.6 %all-reduce.2.cloned.1.call-start = ((), (), s32[]{:S(2)}) async-start(), calls=%async_computation.4 | async-start | bytes 1048576 | tf_op jit(solution)/shard_map/psum | solution.py:76
  61.8 5.7 %copy-start.11 = (s32[1,1,32]{2,1,0:T(1,128)S(1)}, s32[1,1,32]{2,1,0:T(1,128)}, u32[]{:S(2)}) copy-start(s32[1,1,32]{2,1,0:T(1,128)} %param.19) | copy-start | bytes 388
  67.5 6.5 %copy-start.5 = (bf16[1,1,256,256]{3,2,1,0:T(8,128)(2,1)S(1)}, bf16[1,1,256,256]{3,2,1,0:T(8,128)(2,1)}, u32[]{:S(2)}) copy-start(bf16[1,1,256,256]{3,2,1,0:T(8,128)(2,1)} %param.15) | copy-start | bytes 393220
  67.5 6.5 %copy-start.9 = (bf16[256,256]{1,0:T(8,128)(2,1)S(1)}, bf16[256,256]{1,0:T(8,128)(2,1)}, u32[]{:S(2)}) copy-start(bf16[256,256]{1,0:T(8,128)(2,1)} %param.16) | copy-start | bytes 393220
  67.5 10.8 %copy-start.10 = (f32[1,1,256,256]{3,2,1,0:T(8,128)S(1)}, f32[1,1,256,256]{3,2,1,0:T(8,128)}, u32[]{:S(2)}) copy-start(f32[1,1,256,256]{3,2,1,0:T(8,128)} %param.26) | copy-start | bytes 786436
  67.6 11.6 %copy-start.8 = (bf16[256,256]{1,0:T(8,128)(2,1)S(1)}, bf16[256,256]{1,0:T(8,128)(2,1)}, u32[]{:S(2)}) copy-start(bf16[256,256]{1,0:T(8,128)(2,1)} %param.17) | copy-start | bytes 393220
  74.0 8.5 %copy-start.6 = (f32[1,1,256,256]{3,2,1,0:T(8,128)S(1)}, f32[1,1,256,256]{3,2,1,0:T(8,128)}, u32[]{:S(2)}) copy-start(f32[1,1,256,256]{3,2,1,0:T(8,128)} %param.29) | copy-start | bytes 786436
  76.3 6.4 %copy-start.3 = (f32[256,256]{1,0:T(8,128)}, f32[256,256]{1,0:T(8,128)S(1)}, u32[]{:S(2)}) copy-start(f32[256,256]{1,0:T(8,128)S(1)} %scatter_custom_fusion.2) | copy-start | bytes 786436
  82.2 254.2 %reduce-scatter.2.cloned.1.call-start = ((), (), s32[]{:S(2)}) async-start(), calls=%async_computation.3 | async-start | bytes 1310720 | tf_op jit(solution)/shard_map/reduce_scatter | solution.py:90
  86.3 5.7 %copy-start.12 = (s32[1,1,32]{2,1,0:T(1,128)S(1)}, s32[1,1,32]{2,1,0:T(1,128)}, u32[]{:S(2)}) copy-start(s32[1,1,32]{2,1,0:T(1,128)} %param.20) | copy-start | bytes 388
  92.1 7.5 %copy-start.4 = (f32[256,256]{1,0:T(8,128)S(1)}, f32[256,256]{1,0:T(8,128)}, u32[]{:S(2)}) copy-start(f32[256,256]{1,0:T(8,128)} %copy-done.3) | copy-start | bytes 786436
  92.1 7.5 %copy-start.7 = (f32[1,1,256,256]{3,2,1,0:T(8,128)S(1)}, f32[1,1,256,256]{3,2,1,0:T(8,128)}, u32[]{:S(2)}) copy-start(f32[1,1,256,256]{3,2,1,0:T(8,128)} %param.29) | copy-start | bytes 786436
  98.6 1.0 copy-start.1
Sparse Core Ops, SparseCore 0:
  82.4 251.9 all-reduce.1
Sparse Core Ops, SparseCore 1:
  99.6 25.6 reduce-scatter.1
where the time goes:
time: 347 us; the launch traced here: 346 us
  waiting for transfers between devices  234 us (67%)
  starting transfers between devices  25.6 us (7%)
  other arithmetic  24 us (7%)
  local copies, waits for them, and re-layouts  22.1 us (6%)
  between operations  16.5 us (5%)
  matrix products  11.9 us (3%)
  blocking collectives  11.5 us (3%)
    psum x1, waiting for transfers between devices, shards(): summed = lax.psum(jnp.stack([grad_self, grad_neigh]), ('graph', 'slab'))  234 us
    all_to_all x1, starting transfers between devices, shards(): lax.all_to_all(back_out, 'graph', split_axis=0, concat_axis=0, tiled=True)  13 us
    scatter-add x2, other arithmetic, tile_products(): return jax.ops.segment_sum(prods, sum_index, num_segments=n_sum)  12.9 us
    all_to_all x1, starting transfers between devices, shards(): lax.all_to_all(outgoing, 'graph', split_axis=0, concat_axis=0, tiled=True)  12.3 us
    all_gather x1, blocking collectives, shards(): group = lax.all_gather(own, 'slab', axis=0, tiled=True)  11.5 us
    select_n x2, local copies, waits for them, and re-layouts, tile_products(): prods = jnp.where(live[:, None, None], prods, 0.0)  11.3 us
    dot_general x2, matrix products, tile_products(): prods = jnp.einsum(form, vals, chosen, preferred_element_type=jnp.float32)  7.44 us
  transfers between devices with their start and end apart: 4, of which 1 were waited for; matrix products, arithmetic and copies ran while one was open for 13% of the time, Pallas kernels for 0%

commit v1 on v0

v1 whole, which is shorter than its diff:
```python
import functools

import jax
import jax.numpy as jnp
from jax import lax
from jax.experimental import pallas as pl
from jax.experimental.pallas import tpu as pltpu
from jax.sharding import PartitionSpec as P

SMOOTHING = 0.7
MESH = pl.DeviceIdType.MESH
XS, ZS, CORES, YS = 4, 8, 2, 4
N_GRAPH = XS * ZS * CORES
BF = jnp.bfloat16
F32 = jnp.float32


def dot(a, b):
    return lax.dot_general(a, b, (((1,), (0,)), ((), ())), preferred_element_type=F32)


def dot_tn(a, b):
    return lax.dot_general(a, b, (((0,), (0,)), ((), ())), preferred_element_type=F32)


def dot_nt(a, b):
    return lax.dot_general(a, b, (((1,), (1,)), ((), ())), preferred_element_type=F32)


def kernel(
    feats, w_self, w_neigh, vals_h, dst, src, count, pp_h, mir, cnt, mas, mom_h, cot_h, pg_h, gmom_h,
    hidden_o, fgrad_o, sp_o, sg_o, wg_o,
    group, ws, wn, vals, pp, pg, mom, cot, gmom,
    msgf, msg, inbox, a_hi, a_lo, at_hi, at_lo, own_t,
    hid_v, fg_v, sp_v, sg_v,
    wbuf, r_a, s_b, acc_a, r_b, s_c, acc_b, r_c, r_d, wfin, wg_v, s_rs, r_rs,
    lsem, osem, ag_s, ag_r, a2a_s, a2a_r, rs_s, rs_r, w_s, w_r,
):
    g = lax.axis_index("graph")
    y = lax.axis_index("slab")
    core = g % 2
    z = (g // 2) % ZS
    x = g // (2 * ZS)

    loads = {}
    for i, (name, s, d) in enumerate([
        ("pp", pp_h, pp), ("pg", pg_h, pg), ("own", feats, group.at[y]), ("vals", vals_h, vals),
        ("ws", w_self, ws), ("wn", w_neigh, wn), ("mom", mom_h, mom), ("gmom", gmom_h, gmom), ("cot", cot_h, cot),
    ]):
        loads[name] = pltpu.make_async_copy(s, d, lsem.at[i])
        loads[name].start()

    barrier = pltpu.get_barrier_semaphore()

    def sig(d, _):
        pl.semaphore_signal(barrier, inc=1, device_id=((g + d) % N_GRAPH, y), device_id_type=MESH)
        return 0

    lax.fori_loop(1, N_GRAPH, sig, 0)
    for d in range(1, YS):
        pl.semaphore_signal(barrier, inc=1, device_id=(g, (y + d) % YS), device_id_type=MESH)

    nk = 4 * N_GRAPH
    cnt_row = jnp.concatenate([cnt[...]] * 4, axis=1)
    slot_row = lax.broadcasted_iota(jnp.int32, (1, nk), 1) // N_GRAPH
    live = slot_row < cnt_row
    mir_row = jnp.concatenate([mir[c : c + 1, :] for c in range(4)], axis=1)
    mas_row = jnp.concatenate([mas[c : c + 1, :] for c in range(4)], axis=1)
    mir_row = jnp.where(live, mir_row, -1)
    rows = lax.broadcasted_iota(jnp.int32, (256, nk), 0)
    s_mir = jnp.where(rows == mir_row, 1.0, 0.0).astype(BF)
    s_mas = jnp.where(rows == mas_row, 1.0, 0.0).astype(BF)

    inbox[g] = jnp.zeros((16, 128), BF)
    for t, (name, buf, one) in enumerate([("pp", pp, s_mir), ("pg", pg, s_mas)]):
        loads[name].wait()
        out = dot_tn(one, buf[...])
        for c in range(4):
            for h in range(2):
                msgf[pl.ds(t * 8 + h * 4 + c, N_GRAPH, stride=16), :] = out[
                    c * N_GRAPH : (c + 1) * N_GRAPH, h * 128 : (h + 1) * 128
                ]
    msg[...] = msgf[...].reshape(N_GRAPH, 16, 128).astype(BF)

    pl.semaphore_wait(barrier, N_GRAPH - 1 + YS - 1)

    ag = []
    for d in range(1, YS):
        cp = pltpu.make_async_remote_copy(
            feats, group.at[y], ag_s.at[d - 1], ag_r.at[d - 1],
            device_id=(g, (y + d) % YS), device_id_type=MESH)
        cp.start()
        ag.append(cp)

    def send(d, _):
        peer = (g + d) % N_GRAPH
        pltpu.make_async_remote_copy(
            msg.at[peer], inbox.at[g], a2a_s, a2a_r, device_id=(peer, y), device_id_type=MESH).start()
        return 0

    lax.fori_loop(1, N_GRAPH, send, 0)

    loads["vals"].wait()
    n_live = count[0, 0]
    cells = []
    for b in range(32):
        cells.append(jnp.where(b < n_live, dst[0, b] * 8 + src[0, b], -1))

    def chunk(r, _):
        row = pl.multiple_of(r * 16, 16)
        acc = [jnp.zeros((16, 128), F32) for _ in range(16)]
        for b in range(32):
            v = vals[b, pl.ds(row, 16), :].astype(F32)
            for k in range(16):
                acc[k] = acc[k] + v * jnp.where(cells[b] == k, 1.0, 0.0)
        for k in range(16):
            dk, m = k // 8, k % 8
            t, col = m // 2, (m % 2) * 128
            hi = acc[k].astype(BF)
            lo = (acc[k] - hi.astype(F32)).astype(BF)
            a_hi[t, pl.ds(pl.multiple_of(dk * 128 + row, 16), 16), col : col + 128] = hi
            a_lo[t, pl.ds(pl.multiple_of(dk * 128 + row, 16), 16), col : col + 128] = lo
        return 0

    lax.fori_loop(0, 8, chunk, 0)

    for t in range(YS):
        at_hi[t] = a_hi[t].T
        at_lo[t] = a_lo[t].T
    loads["own"].wait()
    own = group[y]
    own_t[...] = own.T
    loads["ws"].wait()
    loads["wn"].wait()
    pre = dot(own, ws[...])
    local = dot(a_hi[y], own) + dot(a_lo[y], own)
    for d in range(1, YS):
        t = (y + YS - d) % YS
        ag[d - 1].wait_recv()
        tile = group[t]
        local = local + dot(a_hi[t], tile) + dot(a_lo[t], tile)

    pltpu.make_async_copy(inbox.at[pl.ds(0, N_GRAPH - 1)], inbox.at[pl.ds(0, N_GRAPH - 1)], a2a_r).wait()
    msgf[...] = inbox[...].astype(F32).reshape(N_GRAPH * 16, 128)
    got = []
    for t in range(2):
        halves = []
        for h in range(2):
            halves.append(jnp.concatenate(
                [msgf[pl.ds(t * 8 + h * 4 + c, N_GRAPH, stride=16), :] for c in range(4)], axis=0))
        got.append(jnp.concatenate(halves, axis=1).astype(BF))
    loads["mom"].wait()
    sp = SMOOTHING * mom[...] + (1.0 - SMOOTHING) * dot(s_mas, got[0])
    sp_v[...] = sp
    outs = [pltpu.make_async_copy(sp_v, sp_o, osem.at[0])]
    outs[-1].start()
    agg = (local + sp).astype(BF)
    pre = pre + dot(agg, wn[...])
    loads["cot"].wait()
    delta = jnp.where(pre > 0, cot[...], jnp.zeros((), BF))
    grads = [dot(own_t[...], delta), dot_tn(agg, delta)]
    for i in range(2):
        for h in range(2):
            wbuf[i, h * 16 : (h + 1) * 16] = grads[i][:, h * 128 : (h + 1) * 128].reshape(16, 16, 128).astype(BF)

    cp_a = pltpu.make_async_remote_copy(
        wbuf.at[1 - core], r_a, w_s.at[0], w_r.at[0], device_id=(g + 1 - 2 * core, y), device_id_type=MESH)
    cp_a.start()

    hid_v[...] = jnp.maximum(pre, 0.0).astype(BF)
    outs.append(pltpu.make_async_copy(hid_v, hidden_o, osem.at[1]))
    outs[-1].start()
    loads["gmom"].wait()
    sg = SMOOTHING * gmom[...] + (1.0 - SMOOTHING) * dot(s_mir, got[1])
    sg_v[...] = sg
    outs.append(pltpu.make_async_copy(sg_v, sg_o, osem.at[2]))
    outs[-1].start()
    gagg = (dot_nt(delta, wn[...]) + sg).astype(BF)
    rs = []
    for d in range(1, YS):
        t = (y + d) % YS
        s_rs[d - 1] = (dot(at_hi[t], gagg) + dot(at_lo[t], gagg)).astype(BF)
        cp = pltpu.make_async_remote_copy(
            s_rs.at[d - 1], r_rs.at[d - 1], rs_s.at[d - 1], rs_r.at[d - 1],
            device_id=(g, t), device_id_type=MESH)
        cp.start()
        rs.append(cp)

    for h in range(2):
        mine = jnp.where(core == 0, grads[0][:, h * 128 : (h + 1) * 128], grads[1][:, h * 128 : (h + 1) * 128])
        acc_a[h * 16 : (h + 1) * 16] = mine.reshape(16, 16, 128)
    cp_a.wait_recv()
    total = acc_a[...] + r_a[...].astype(F32)
    acc_a[...] = total
    s_b[...] = total.astype(BF)
    ops = [cp_a]

    hop = []
    for d in range(1, XS):
        px = (x + d) % XS
        cp = pltpu.make_async_remote_copy(
            s_b.at[pl.ds(px * 8, 8)], r_b.at[d - 1], w_s.at[d], w_r.at[d],
            device_id=(px * 2 * ZS + z * 2 + core, y), device_id_type=MESH)
        cp.start()
        hop.append(cp)
    fg = dot_nt(delta, ws[...]) + dot(at_hi[y], gagg) + dot(at_lo[y], gagg)
    for cp in hop:
        cp.wait_recv()
    ops += hop
    total = acc_a[pl.ds(x * 8, 8)]
    for d in range(1, XS):
        total = total + r_b[d - 1].astype(F32)
    acc_b[...] = total
    s_c[...] = total.astype(BF)

    hop = []
    for d in range(1, ZS):
        pz = (z + d) % ZS
        cp = pltpu.make_async_remote_copy(
            s_c.at[pz], r_c.at[d - 1], w_s.at[3 + d], w_r.at[3 + d],
            device_id=(x * 2 * ZS + pz * 2 + core, y), device_id_type=MESH)
        cp.start()
        hop.append(cp)
    for cp in hop:
        cp.wait_recv()
    ops += hop
    total = acc_b[z]
    for d in range(1, ZS):
        total = total + r_c[d - 1].astype(F32)
    r_d[y] = total

    hop = []
    for d in range(1, YS):
        cp = pltpu.make_async_remote_copy(
            r_d.at[y], r_d.at[y], w_s.at[10 + d], w_r.at[10 + d],
            device_id=(g, (y + d) % YS), device_id_type=MESH)
        cp.start()
        hop.append(cp)
    for cp in hop:
        cp.wait_recv()
    ops += hop
    total = ((r_d[0] + r_d[1]) + r_d[2]) + r_d[3]
    wfin[core, x * 8 + z] = total.astype(BF)

    hop = []
    for d in range(1, ZS):
        pz = (z + d) % ZS
        here = wfin.at[core, x * 8 + z]
        cp = pltpu.make_async_remote_copy(
            here, here, w_s.at[13 + d], w_r.at[13 + d],
            device_id=(x * 2 * ZS + pz * 2 + core, y), device_id_type=MESH)
        cp.start()
        hop.append(cp)
    for cp in hop:
        cp.wait_recv()
    ops += hop
    hop = []
    for d in range(1, XS):
        px = (x + d) % XS
        here = wfin.at[core, pl.ds(x * 8, 8)]
        cp = pltpu.make_async_remote_copy(
            here, here, w_s.at[20 + d], w_r.at[20 + d],
            device_id=(px * 2 * ZS + z * 2 + core, y), device_id_type=MESH)
        cp.start()
        hop.append(cp)
    for cp in hop:
        cp.wait_recv()
    ops += hop
    here = wfin.at[core]
    last = pltpu.make_async_remote_copy(
        here, here, w_s.at[24], w_r.at[24], device_id=(g + 1 - 2 * core, y), device_id_type=MESH)
    last.start()
    ops.append(last)

    for cp in rs:
        cp.wait_recv()
    for d in range(1, YS):
        fg = fg + r_rs[d - 1].astype(F32)
    fg_v[...] = fg.astype(BF)
    outs.append(pltpu.make_async_copy(fg_v, fgrad_o, osem.at[3]))
    outs[-1].start()

    last.wait_recv()
    scale = 1.0 / (N_GRAPH * YS * 256) ** 0.5
    for i in range(2):
        for h in range(2):
            wg_v[i, :, h * 128 : (h + 1) * 128] = (
                wfin[i, h * 16 : (h + 1) * 16].astype(F32).reshape(256, 128) * scale)
    outs.append(pltpu.make_async_copy(wg_v, wg_o, osem.at[4]))
    outs[-1].start()

    for cp in ag + rs + ops:
        cp.wait_send()
    pltpu.make_async_copy(msg.at[pl.ds(0, N_GRAPH - 1)], msg.at[pl.ds(0, N_GRAPH - 1)], a2a_s).wait()
    for cp in outs:
        cp.wait()


def shards(
    feats, w_self, w_neigh, block_vals, block_dst, block_src, block_count, prev_partial,
    mirror_rows, send_count, master_rows, momentum, cotangent, prev_grad, grad_momentum,
):
    sds = jax.ShapeDtypeStruct
    hbm = pl.BlockSpec(memory_space=pl.ANY)
    vm = pl.BlockSpec(memory_space=pltpu.VMEM)
    sm = pl.BlockSpec(memory_space=pltpu.SMEM)
    V = pltpu.VMEM
    dma = pltpu.SemaphoreType.DMA
    mat = lambda dt: V((256, 256), dt)
    hidden, fgrad, sp, sg, wg = pl.pallas_call(
        kernel,
        out_shape=(
            sds((256, 256), BF), sds((256, 256), BF), sds((256, 256), F32), sds((256, 256), F32),
            sds((2, 256, 256), F32),
        ),
        in_specs=[hbm, hbm, hbm, hbm, sm, sm, sm, hbm, vm, vm, vm, hbm, hbm, hbm, hbm],
        out_specs=[hbm] * 5,
        scratch_shapes=[
            V((YS, 256, 256), BF), mat(BF), mat(BF), V((32, 128, 128), BF), mat(BF), mat(BF), mat(F32), mat(BF), mat(F32),
            V((N_GRAPH * 16, 128), F32), V((N_GRAPH, 16, 128), BF), V((N_GRAPH, 16, 128), BF),
            V((YS, 256, 256), BF), V((YS, 256, 256), BF), V((YS, 256, 256), BF), V((YS, 256, 256), BF), mat(BF),
            mat(BF), mat(BF), mat(F32), mat(F32),
            V((2, 32, 16, 128), BF), V((32, 16, 128), BF), V((32, 16, 128), BF), V((32, 16, 128), F32),
            V((XS - 1, 8, 16, 128), BF), V((8, 16, 128), BF), V((8, 16, 128), F32), V((ZS - 1, 16, 128), BF),
            V((YS, 16, 128), F32), V((2, 32, 16, 128), BF), V((2, 256, 256), F32),
            V((YS - 1, 256, 256), BF), V((YS - 1, 256, 256), BF),
            dma((9,)), dma((5,)), dma((YS - 1,)), dma((YS - 1,)), dma, dma, dma((YS - 1,)), dma((YS - 1,)),
            dma((25,)), dma((25,)),
        ],
        compiler_params=pltpu.CompilerParams(
            collective_id=0, has_side_effects=True, vmem_limit_bytes=62 * 1024 * 1024),
    )(
        feats[0, 0], w_self, w_neigh, block_vals[0, 0], block_dst[0], block_src[0], block_count,
        prev_partial[0, 0], jnp.swapaxes(mirror_rows[0, 0], 0, 1), send_count[0], jnp.swapaxes(master_rows[0, 0], 0, 1),
        momentum[0, 0], cotangent[0, 0], prev_grad[0, 0], grad_momentum[0, 0],
    )
    return hidden[None, None], fgrad[None, None], sp[None, None], sg[None, None], wg


def solution(mesh):
    gs = lambda n: P("graph", "slab", *([None] * n))
    in_specs = (
        gs(2), P(), P(), gs(3), gs(1), gs(1), gs(0), gs(2), gs(2), gs(1), gs(2), gs(2), gs(2), gs(2), gs(2),
    )
    out_specs = (gs(2), gs(2), gs(2), gs(2), P())
    return jax.shard_map(shards, mesh=mesh, in_specs=in_specs, out_specs=out_specs, check_vma=False)
```

time: 347 us -> 54 us (0.16)
  waiting for transfers between devices: 234 us -> 0 us
  Pallas kernels: 0 us -> 48.1 us
  starting transfers between devices: 25.6 us -> 0 us
  other arithmetic: 24 us -> 0 us
  local copies, waits for them, and re-layouts: 22.1 us -> 4.49 us
  between operations: 16.5 us -> 1.31 us
  matrix products: 11.9 us -> 0 us
  blocking collectives: 11.5 us -> 0 us
    psum x1 -> x0, waiting for transfers between devices: 234 us -> none  [shards(): summed = lax.psum(jnp.stack([grad_self, grad_neigh]), ('graph', 'slab'))]
    pallas_call x0 -> x1, Pallas kernels: none -> 48.1 us  [shards(): pl.pallas_call(kernel, out_shape=(sds((256, 256), BF), sds((256, 256), BF...]
    all_to_all x2 -> x0, starting transfers between devices: 25.3 us -> none  [the longest x1 13 us: shards(): lax.all_to_all(back_out, 'graph', split_axis=0, concat_axis=0, tiled=True)]
    scatter-add x4 -> x0, other arithmetic: 16.9 us -> none  [the longest x2 12.9 us: tile_products(): return jax.ops.segment_sum(prods, sum_index, num_segments=n_sum)]
    dot_general x8 -> x0, matrix products: 11.9 us -> none  [the longest x2 7.44 us: tile_products(): prods = jnp.einsum(form, vals, chosen, preferred_element_type=jnp.float32)]
    select_n x6 -> x0, local copies, waits for them, and re-layouts: 11.7 us -> none  [the longest x2 11.3 us: tile_products(): prods = jnp.where(live[:, None, None], prods, 0.0)]
    all_gather x1 -> x0, blocking collectives: 11.5 us -> none  [shards(): group = lax.all_gather(own, 'slab', axis=0, tiled=True)]
    gather x6 -> x0, local copies, waits for them, and re-layouts: 6.45 us -> none  [the longest x2 2.68 us: tile_products(): chosen = tiles[pick_index]]
  transfers between devices with their start and end apart: 4 -> 0, of which waited for: 1 -> 0; matrix products, arithmetic and copies ran while one was open for 13% -> 0% of each run, Pallas kernels for 0% -> 0%
where the time goes in v1:
time: 54 us; the launch traced here: 53.9 us
  Pallas kernels  48.1 us (89%)
  local copies, waits for them, and re-layouts  4.49 us (8%)
  between operations  1.31 us (2%)
    pallas_call x1, Pallas kernels, shards(): pl.pallas_call(kernel, out_shape=(sds((256, 256), BF), sds((256, 256), BF...  48.1 us
    unnamed x13, local copies, waits for them, and re-layouts  4.49 us

profile of v1, /device:TPU:1, one launch (start us, length us, event | category | flops | bytes accessed | tf_op | source)
XLA Modules:
  0.0 53.9 jit_solution(15440456756958791977)
XLA Ops:
  1.3 48.1 %shard_map.182 = (bf16[256,256]{1,0:T(8,128)(2,1)}, bf16[256,256]{1,0:T(8,128)(2,1)}, f32[256,256]{1,0:T(8,128)}, f32[256,256]{1,0:T(8,128)}, f32[2,256,256]{2,1,0:T(8,128)}) custom-call(bf16[256,256]{1,0:T(8,128)(2,1)} %bitcast.27, bf16[256,256]{1,0:T(8,128)(2,1)} %w_self.1, bf16[256,256]{1,0:T(8,128)(2,1)} %w_neigh.1, bf16[32,128,128]{2,1,0:T(8,128)(2,1)} %bitcast.20, ...), custom_call_target="tpu_custom_call" | custom-call | tf_op jit(solution)/shard_map/pallas_call | solution.py:310
  49.4 0.0 copy-start.3
  49.4 0.0 copy-start.2
  49.4 1.6 %copy.26 = bf16[1,1,256,256]{3,2,1,0:T(8,128)(2,1)} copy(bf16[1,1,256,256]{3,2,1,0:T(8,128)(2,1)} %bitcast.26) | data formatting | bytes 262144
  51.0 0.0 copy-done.3
  51.0 0.0 copy-start.1
  51.0 0.7 %copy.27 = bf16[1,1,256,256]{3,2,1,0:T(8,128)(2,1)} copy(bf16[1,1,256,256]{3,2,1,0:T(8,128)(2,1)S(1)} %bitcast.25) | data formatting | bytes 262144
  51.7 0.0 copy-done.2
  51.7 0.0 copy-start
  51.7 0.7 %copy.28 = f32[1,1,256,256]{3,2,1,0:T(8,128)} copy(f32[1,1,256,256]{3,2,1,0:T(8,128)S(1)} %bitcast.22) | data formatting | bytes 524288
  52.4 0.0 copy-done.1
  52.4 0.7 %copy.29 = f32[1,1,256,256]{3,2,1,0:T(8,128)} copy(f32[1,1,256,256]{3,2,1,0:T(8,128)S(1)} %bitcast.21) | data formatting | bytes 524288
  53.1 0.0 copy-done
  53.1 0.8 %copy.30 = f32[2,256,256]{2,1,0:T(8,128)} copy(f32[2,256,256]{2,1,0:T(8,128)S(1)} %copy-done) | data formatting | bytes 1048576
Async XLA Ops:
  49.4 1.6 %copy-start.3 = (bf16[256,256]{1,0:T(8,128)(2,1)S(1)}, bf16[256,256]{1,0:T(8,128)(2,1)}, u32[]{:S(2)}) copy-start(bf16[256,256]{1,0:T(8,128)(2,1)} %get-tuple-element.11) | copy-start | bytes 393220
  49.4 2.3 %copy-start.2 = (f32[256,256]{1,0:T(8,128)S(1)}, f32[256,256]{1,0:T(8,128)}, u32[]{:S(2)}) copy-start(f32[256,256]{1,0:T(8,128)} %get-tuple-element.12) | copy-start | bytes 786436
  51.0 1.4 %copy-start.1 = (f32[256,256]{1,0:T(8,128)S(1)}, f32[256,256]{1,0:T(8,128)}, u32[]{:S(2)}) copy-start(f32[256,256]{1,0:T(8,128)} %get-tuple-element.13) | copy-start | bytes 786436
  51.7 1.4 %copy-start = (f32[2,256,256]{2,1,0:T(8,128)S(1)}, f32[2,256,256]{2,1,0:T(8,128)}, u32[]{:S(2)}) copy-start(f32[2,256,256]{2,1,0:T(8,128)} %get-tuple-element.24) | copy-start | bytes 1572868

commit v2 on v1

v2 whole, which is shorter than its diff:
```python
import functools

import jax
import jax.numpy as jnp
from jax import lax
from jax.experimental import pallas as pl
from jax.experimental.pallas import tpu as pltpu
from jax.sharding import PartitionSpec as P

SMOOTHING = 0.7
MESH = pl.DeviceIdType.MESH
XS, ZS, CORES, YS = 4, 8, 2, 4
N_GRAPH = XS * ZS * CORES
CHIPS = XS * ZS
BF = jnp.bfloat16
F32 = jnp.float32


def dot(a, b):
    return lax.dot_general(a, b, (((1,), (0,)), ((), ())), preferred_element_type=F32)


def dot_tn(a, b):
    return lax.dot_general(a, b, (((0,), (0,)), ((), ())), preferred_element_type=F32)


def dot_nt(a, b):
    return lax.dot_general(a, b, (((1,), (1,)), ((), ())), preferred_element_type=F32)


def kernel(
    feats, w_self, w_neigh, vals_h, dst, src, count, pp_h, mir, cnt, mas, mom_h, cot_h, pg_h, gmom_h,
    hidden_o, fgrad_o, sp_o, sg_o, wg_o,
    group, ws, wn, vals, pp, pg, mom, cot, gmom,
    msgf, msg, inbox, a_hi, a_lo, at_hi, at_lo,
    hid_v, fg_v, sp_v, sg_v,
    s_a, r_a, s_b, acc_a, r_b, r_c, wfin, wg_v, s_rs, r_rs,
    lsem, osem, ag_s, ag_r, a2a_s, a2a_r, fw_s, fw_r, rs_s, rs_r, w_s, w_r,
):
    g = lax.axis_index("graph")
    y = lax.axis_index("slab")
    core = g % 2
    chip = g // 2
    z = chip % ZS
    x = chip // ZS
    sibling = (g + 1 - 2 * core, y)
    plane = [(dx, dy) for dx in range(XS) for dy in range(YS) if dx or dy]

    def at_plane(dx, dy):
        return ((x + dx) % XS, (y + dy) % YS)

    def device(px, pz, py):
        return ((px * ZS + pz) * 2 + core, py)

    loads = {}
    for i, (name, s, d) in enumerate([
        ("pp", pp_h, pp), ("pg", pg_h, pg), ("own", feats, group.at[y]), ("vals", vals_h, vals),
        ("ws", w_self, ws), ("wn", w_neigh, wn), ("mom", mom_h, mom), ("gmom", gmom_h, gmom), ("cot", cot_h, cot),
    ]):
        loads[name] = pltpu.make_async_copy(s, d, lsem.at[i])
        loads[name].start()

    barrier = pltpu.get_barrier_semaphore()

    def greet(peer):
        pl.semaphore_signal(barrier, inc=1, device_id=peer, device_id_type=MESH)

    def sig(d, _):
        greet((((chip + d) % CHIPS) * 2 + core, y))
        return 0

    lax.fori_loop(1, CHIPS, sig, 0)
    greet(sibling)
    away = [(dx, dy) for dx, dy in plane if dy]
    for dx, dy in away:
        px, py = at_plane(dx, dy)
        greet(device(px, z, py))

    nk = 4 * N_GRAPH
    cnt_row = jnp.concatenate([cnt[...]] * 4, axis=1)
    slot_row = lax.broadcasted_iota(jnp.int32, (1, nk), 1) // N_GRAPH
    live = slot_row < cnt_row
    mir_row = jnp.concatenate([mir[c : c + 1, :] for c in range(4)], axis=1)
    mas_row = jnp.concatenate([mas[c : c + 1, :] for c in range(4)], axis=1)
    mir_row = jnp.where(live, mir_row, -1)
    rows = lax.broadcasted_iota(jnp.int32, (256, nk), 0)
    s_mir = jnp.where(rows == mir_row, 1.0, 0.0).astype(BF)
    s_mas = jnp.where(rows == mas_row, 1.0, 0.0).astype(BF)

    for t, (name, buf, one) in enumerate([("pp", pp, s_mir), ("pg", pg, s_mas)]):
        loads[name].wait()
        out = dot_tn(one, buf[...])
        for c in range(4):
            for h in range(2):
                msgf[t, pl.ds(h * 4 + c, N_GRAPH, stride=8), :] = out[
                    c * N_GRAPH : (c + 1) * N_GRAPH, h * 128 : (h + 1) * 128
                ]
        msg[t] = msgf[t].reshape(CHIPS, 16, 128).astype(BF)
        inbox[t, chip, core] = msg[t, chip]

    pl.semaphore_wait(barrier, CHIPS + len(away))

    ag = []
    for d in range(1, YS):
        cp = pltpu.make_async_remote_copy(
            feats, group.at[y], ag_s.at[d - 1], ag_r.at[d - 1],
            device_id=(g, (y + d) % YS), device_id_type=MESH)
        cp.start()
        ag.append(cp)

    for t in range(2):

        def send(d, _):
            peer = (chip + d) % CHIPS
            pltpu.make_async_remote_copy(
                msg.at[t, peer], inbox.at[t, chip, core], a2a_s.at[t], a2a_r.at[t],
                device_id=(peer * 2 + core, y), device_id_type=MESH).start()
            return 0

        lax.fori_loop(1, CHIPS, send, 0)

    def forward(t):
        some = inbox.at[t, pl.ds(0, CHIPS - 1), 0]
        pltpu.make_async_copy(some, some, a2a_r.at[t]).wait()
        cp = pltpu.make_async_remote_copy(
            inbox.at[t, :, core], inbox.at[t, :, core], fw_s.at[t], fw_r.at[t],
            device_id=sibling, device_id_type=MESH)
        cp.start()
        return cp

    def received(t):
        both = inbox[t].astype(F32).reshape(N_GRAPH, 16, 128)
        msgf[t] = jnp.where(core == 0, both[:, :8], both[:, 8:]).reshape(N_GRAPH * 8, 128)
        halves = []
        for h in range(2):
            halves.append(jnp.concatenate(
                [msgf[t, pl.ds(h * 4 + c, N_GRAPH, stride=8), :] for c in range(4)], axis=0))
        return jnp.concatenate(halves, axis=1).astype(BF)

    loads["vals"].wait()
    n_live = count[0, 0]
    cells = []
    for b in range(32):
        cells.append(jnp.where(b < n_live, dst[0, b] * 8 + src[0, b], -1))

    def chunk(r, _):
        row = pl.multiple_of(r * 16, 16)
        acc = [jnp.zeros((16, 128), F32) for _ in range(16)]
        for b in range(32):
            v = vals[b, pl.ds(row, 16), :].astype(F32)
            for k in range(16):
                acc[k] = acc[k] + v * jnp.where(cells[b] == k, 1.0, 0.0)
        for k in range(16):
            dk, m = k // 8, k % 8
            t, col = m // 2, (m % 2) * 128
            hi = acc[k].astype(BF)
            lo = (acc[k] - hi.astype(F32)).astype(BF)
            a_hi[t, pl.ds(pl.multiple_of(dk * 128 + row, 16), 16), col : col + 128] = hi
            a_lo[t, pl.ds(pl.multiple_of(dk * 128 + row, 16), 16), col : col + 128] = lo
        return 0

    lax.fori_loop(0, 8, chunk, 0)

    for t in range(YS):
        at_hi[t] = a_hi[t].T
        at_lo[t] = a_lo[t].T
    loads["own"].wait()
    own = group[y]
    loads["ws"].wait()
    loads["wn"].wait()
    pre = dot(own, ws[...])
    local = dot(a_hi[y], own) + dot(a_lo[y], own)
    for d in range(1, YS):
        t = (y + YS - d) % YS
        ag[d - 1].wait_recv()
        tile = group[t]
        local = local + dot(a_hi[t], tile) + dot(a_lo[t], tile)

    fw = [forward(0)]
    loads["mom"].wait()
    loads["cot"].wait()
    fw[0].wait_recv()
    sp = SMOOTHING * mom[...] + (1.0 - SMOOTHING) * dot(s_mas, received(0))
    agg = (local + sp).astype(BF)
    pre = pre + dot(agg, wn[...])
    delta = jnp.where(pre > 0, cot[...], jnp.zeros((), BF))

    def tiles(m, h):
        return m[:, h * 128 : (h + 1) * 128].reshape(16, 16, 128)

    given = dot_tn(jnp.where(core == 0, agg, own), delta)
    for h in range(2):
        s_a[h * 16 : (h + 1) * 16] = tiles(given, h).astype(BF)
    cp_a = pltpu.make_async_remote_copy(
        s_a, r_a, w_s.at[0], w_r.at[0], device_id=sibling, device_id_type=MESH)
    cp_a.start()
    fw.append(forward(1))
    kept = dot_tn(jnp.where(core == 0, own, agg), delta)
    cp_a.wait_recv()
    for h in range(2):
        part = slice(h * 16, (h + 1) * 16)
        total = tiles(kept, h) + r_a[part].astype(F32)
        acc_a[part] = total
        s_b[part] = total.astype(BF)
    ops = [cp_a]

    place = x * YS + y
    hop = []
    for i, (dx, dy) in enumerate(plane):
        px, py = at_plane(dx, dy)
        cp = pltpu.make_async_remote_copy(
            s_b.at[pl.ds((px * YS + py) * 2, 2)], r_b.at[i], w_s.at[1 + i], w_r.at[1 + i],
            device_id=device(px, z, py), device_id_type=MESH)
        cp.start()
        hop.append(cp)

    sp_v[...] = sp
    outs = [pltpu.make_async_copy(sp_v, sp_o, osem.at[0])]
    outs[-1].start()
    hid_v[...] = jnp.maximum(pre, 0.0).astype(BF)
    outs.append(pltpu.make_async_copy(hid_v, hidden_o, osem.at[1]))
    outs[-1].start()
    loads["gmom"].wait()
    fw[1].wait_recv()
    sg = SMOOTHING * gmom[...] + (1.0 - SMOOTHING) * dot(s_mir, received(1))
    sg_v[...] = sg
    outs.append(pltpu.make_async_copy(sg_v, sg_o, osem.at[2]))
    outs[-1].start()
    gagg = (dot_nt(delta, wn[...]) + sg).astype(BF)
    rs = []
    for d in range(1, YS):
        t = (y + d) % YS
        s_rs[d - 1] = (dot(at_hi[t], gagg) + dot(at_lo[t], gagg)).astype(BF)
        cp = pltpu.make_async_remote_copy(
            s_rs.at[d - 1], r_rs.at[d - 1], rs_s.at[d - 1], rs_r.at[d - 1],
            device_id=(g, t), device_id_type=MESH)
        cp.start()
        rs.append(cp)

    for cp in hop:
        cp.wait_recv()
    ops += hop
    total = acc_a[pl.ds(place * 2, 2)]
    for i in range(len(plane)):
        total = total + r_b[i].astype(F32)

    r_c[z] = total.astype(BF)
    hop = []
    for d in range(1, ZS):
        cp = pltpu.make_async_remote_copy(
            r_c.at[z], r_c.at[z], w_s.at[15 + d], w_r.at[15 + d],
            device_id=device(x, (z + d) % ZS, y), device_id_type=MESH)
        cp.start()
        hop.append(cp)
    fg = dot_nt(delta, ws[...]) + dot(at_hi[y], gagg) + dot(at_lo[y], gagg)
    for cp in hop:
        cp.wait_recv()
    ops += hop
    total = r_c[0].astype(F32)
    for i in range(1, ZS):
        total = total + r_c[i].astype(F32)
    mine = wfin.at[core, pl.ds(place * 2, 2)]
    mine[...] = total.astype(BF)

    hop = []
    for i, (dx, dy) in enumerate(plane):
        px, py = at_plane(dx, dy)
        cp = pltpu.make_async_remote_copy(
            mine, mine, w_s.at[23 + i], w_r.at[23 + i], device_id=device(px, z, py), device_id_type=MESH)
        cp.start()
        hop.append(cp)
    for cp in rs:
        cp.wait_recv()
    for d in range(1, YS):
        fg = fg + r_rs[d - 1].astype(F32)
    fg_v[...] = fg.astype(BF)
    outs.append(pltpu.make_async_copy(fg_v, fgrad_o, osem.at[3]))
    outs[-1].start()

    for cp in hop:
        cp.wait_recv()
    ops += hop
    last = pltpu.make_async_remote_copy(
        wfin.at[core], wfin.at[core], w_s.at[38], w_r.at[38], device_id=sibling, device_id_type=MESH)
    last.start()
    ops.append(last)
    last.wait_recv()
    scale = 1.0 / (N_GRAPH * YS * 256) ** 0.5
    for i in range(2):
        for h in range(2):
            wg_v[i, :, h * 128 : (h + 1) * 128] = (
                wfin[i, h * 16 : (h + 1) * 16].astype(F32).reshape(256, 128) * scale)
    outs.append(pltpu.make_async_copy(wg_v, wg_o, osem.at[4]))
    outs[-1].start()

    for cp in ag + fw + rs + ops:
        cp.wait_send()
    for t in range(2):
        some = msg.at[t, pl.ds(0, CHIPS - 1)]
        pltpu.make_async_copy(some, some, a2a_s.at[t]).wait()
    for cp in outs:
        cp.wait()


def hand_over(*refs):
    results, outs, stage, sem = refs[:5], refs[5:10], refs[10:15], refs[15]
    order = (4, 2, 3, 0, 1)
    pull = [pltpu.make_async_copy(results[i], stage[i], sem.at[i]) for i in range(5)]
    push = [pltpu.make_async_copy(stage[i], outs[i], sem.at[5 + i]) for i in range(5)]
    for i in order:
        pull[i].start()
    for i in order:
        pull[i].wait()
        push[i].start()
    for i in order:
        push[i].wait()


def shards(
    feats, w_self, w_neigh, block_vals, block_dst, block_src, block_count, prev_partial,
    mirror_rows, send_count, master_rows, momentum, cotangent, prev_grad, grad_momentum,
):
    sds = jax.ShapeDtypeStruct
    hbm = pl.BlockSpec(memory_space=pl.ANY)
    vm = pl.BlockSpec(memory_space=pltpu.VMEM)
    sm = pl.BlockSpec(memory_space=pltpu.SMEM)
    V = pltpu.VMEM
    dma = pltpu.SemaphoreType.DMA
    mat = lambda dt: V((256, 256), dt)
    results = pl.pallas_call(
        kernel,
        out_shape=(
            sds((256, 256), BF), sds((256, 256), BF), sds((256, 256), F32), sds((256, 256), F32),
            sds((2, 256, 256), F32),
        ),
        in_specs=[hbm, hbm, hbm, hbm, sm, sm, sm, hbm, vm, vm, vm, hbm, hbm, hbm, hbm],
        out_specs=[hbm] * 5,
        scratch_shapes=[
            V((YS, 256, 256), BF), mat(BF), mat(BF), V((32, 128, 128), BF), mat(BF), mat(BF), mat(F32), mat(BF), mat(F32),
            V((2, N_GRAPH * 8, 128), F32), V((2, CHIPS, 16, 128), BF), V((2, CHIPS, CORES, 16, 128), BF),
            V((YS, 256, 256), BF), V((YS, 256, 256), BF), V((YS, 256, 256), BF), V((YS, 256, 256), BF),
            mat(BF), mat(BF), mat(F32), mat(F32),
            V((32, 16, 128), BF), V((32, 16, 128), BF), V((32, 16, 128), BF), V((32, 16, 128), F32),
            V((XS * YS - 1, 2, 16, 128), BF), V((ZS, 2, 16, 128), BF), V((2, 32, 16, 128), BF), V((2, 256, 256), F32),
            V((YS - 1, 256, 256), BF), V((YS - 1, 256, 256), BF),
            dma((9,)), dma((5,)), dma((YS - 1,)), dma((YS - 1,)), dma((2,)), dma((2,)), dma((2,)), dma((2,)),
            dma((YS - 1,)), dma((YS - 1,)), dma((39,)), dma((39,)),
        ],
        compiler_params=pltpu.CompilerParams(
            collective_id=0, has_side_effects=True, vmem_limit_bytes=62 * 1024 * 1024),
    )(
        feats[0, 0], w_self, w_neigh, block_vals[0, 0], block_dst[0], block_src[0], block_count,
        prev_partial[0, 0], jnp.swapaxes(mirror_rows[0, 0], 0, 1), send_count[0], jnp.swapaxes(master_rows[0, 0], 0, 1),
        momentum[0, 0], cotangent[0, 0], prev_grad[0, 0], grad_momentum[0, 0],
    )
    hidden, fgrad, sp, sg, wg = pl.pallas_call(
        hand_over,
        out_shape=tuple(sds(r.shape, r.dtype) for r in results),
        in_specs=[hbm] * 5,
        out_specs=[hbm] * 5,
        scratch_shapes=[V(r.shape, r.dtype) for r in results] + [dma((10,))],
        compiler_params=pltpu.CompilerParams(vmem_limit_bytes=62 * 1024 * 1024),
    )(*results)
    return hidden[None, None], fgrad[None, None], sp[None, None], sg[None, None], wg


def solution(mesh):
    gs = lambda n: P("graph", "slab", *([None] * n))
    in_specs = (
        gs(2), P(), P(), gs(3), gs(1), gs(1), gs(0), gs(2), gs(2), gs(1), gs(2), gs(2), gs(2), gs(2), gs(2),
    )
    out_specs = (gs(2), gs(2), gs(2), gs(2), P())
    return jax.shard_map(shards, mesh=mesh, in_specs=in_specs, out_specs=out_specs, check_vma=False)
```

time: 54 us -> 45.8 us (0.85)
  local copies, waits for them, and re-layouts: 4.49 us -> 0 us
  Pallas kernels: 48.1 us -> 44.4 us
    pallas_call x1, Pallas kernels: 48.1 us -> 42.2 us  [shards(): pl.pallas_call(kernel, out_shape=(sds((256, 256), BF), sds((256, 256), BF...]
    unnamed x13 -> x0, local copies, waits for them, and re-layouts: 4.49 us -> none
    pallas_call x0 -> x1, Pallas kernels: none -> 2.17 us  [shards(): pl.pallas_call(hand_over, out_shape=tuple((sds(r.shape, r.dtype) for r in...]
where the time goes in v2:
time: 45.8 us; the launch traced here: 45.7 us
  Pallas kernels  44.4 us (97%)
  between operations  1.29 us (3%)
    pallas_call x1, Pallas kernels, shards(): pl.pallas_call(kernel, out_shape=(sds((256, 256), BF), sds((256, 256), BF...  42.2 us
    pallas_call x1, Pallas kernels, shards(): pl.pallas_call(hand_over, out_shape=tuple((sds(r.shape, r.dtype) for r in...  2.17 us

profile of v2, /device:TPU:1, one launch (start us, length us, event | category | flops | bytes accessed | tf_op | source)
XLA Modules:
  0.0 45.7 jit_solution(2948673085014628348)
XLA Ops:
  1.3 42.2 %shard_map.182 = (bf16[256,256]{1,0:T(8,128)(2,1)}, bf16[256,256]{1,0:T(8,128)(2,1)}, f32[256,256]{1,0:T(8,128)}, f32[256,256]{1,0:T(8,128)}, f32[2,256,256]{2,1,0:T(8,128)}) custom-call(bf16[256,256]{1,0:T(8,128)(2,1)} %bitcast.23, bf16[256,256]{1,0:T(8,128)(2,1)} %w_self.1, bf16[256,256]{1,0:T(8,128)(2,1)} %w_neigh.1, bf16[32,128,128]{2,1,0:T(8,128)(2,1)} %bitcast.20, ...), custom_call_target="tpu_custom_call" | custom-call | tf_op jit(solution)/shard_map/pallas_call | solution.py:330
  43.5 2.2 %shard_map.183 = (bf16[256,256]{1,0:T(8,128)(2,1)}, bf16[256,256]{1,0:T(8,128)(2,1)}, f32[256,256]{1,0:T(8,128)}, f32[256,256]{1,0:T(8,128)}, f32[2,256,256]{2,1,0:T(8,128)}) custom-call(bf16[256,256]{1,0:T(8,128)(2,1)} %get-tuple-element.15.refs_0_, bf16[256,256]{1,0:T(8,128)(2,1)} %get-tuple-element.16.refs_1_, f32[256,256]{1,0:T(8,128)} %get-tuple-element.17.refs_2_, ...), custom_call_target="tpu_custom_call" | custom-call | tf_op jit(solution)/shard_map/pallas_call | solution.py:356

commit v3 on v2

--- a/solution.py
+++ b/solution.py
@@ -14,6 +14,7 @@
 CHIPS = XS * ZS
 BF = jnp.bfloat16
 F32 = jnp.float32
+I32 = jnp.int32
 
 
 def dot(a, b):
@@ -29,12 +30,12 @@
 
 
 def kernel(
-    feats, w_self, w_neigh, vals_h, dst, src, count, pp_h, mir, cnt, mas, mom_h, cot_h, pg_h, gmom_h,
+    feats, w_self, w_neigh, vals_h, dst_h, src_h, count_h, pp_h, mir_h, cnt_h, mas_h, mom_h, cot_h, pg_h, gmom_h,
     hidden_o, fgrad_o, sp_o, sg_o, wg_o,
-    group, ws, wn, vals, pp, pg, mom, cot, gmom,
+    group, ws, wn, vals, pp, pg, mom, cot, gmom, mir, mas, cnt, dst, src, count,
     msgf, msg, inbox, a_hi, a_lo, at_hi, at_lo,
     hid_v, fg_v, sp_v, sg_v,
-    s_a, r_a, s_b, acc_a, r_b, r_c, wfin, wg_v, s_rs, r_rs,
+    s_a, r_a, s_b, acc_a, r_b, r_c, wfin, s_rs, r_rs,
     lsem, osem, ag_s, ag_r, a2a_s, a2a_r, fw_s, fw_r, rs_s, rs_r, w_s, w_r,
 ):
     g = lax.axis_index("graph")
@@ -44,7 +45,16 @@
     z = chip % ZS
     x = chip // ZS
     sibling = (g + 1 - 2 * core, y)
+    def near(d, n):
+        return min(d, n - d)
+
     plane = [(dx, dy) for dx in range(XS) for dy in range(YS) if dx or dy]
+    plane.sort(key=lambda o: -near(o[0], XS) - near(o[1], YS))
+    sheet = [(dx, dz) for dx in range(XS) for dz in range(ZS) if dx or dz]
+    sheet.sort(key=lambda o: -near(o[0], XS) - near(o[1], ZS))
+    line = sorted(range(1, ZS), key=lambda d: -near(d, ZS))
+    slabs = sorted(range(1, YS), key=lambda d: -near(d, YS))
+
 
     def at_plane(dx, dy):
         return ((x + dx) % XS, (y + dy) % YS)
@@ -52,30 +62,30 @@
     def device(px, pz, py):
         return ((px * ZS + pz) * 2 + core, py)
 
-    loads = {}
-    for i, (name, s, d) in enumerate([
-        ("pp", pp_h, pp), ("pg", pg_h, pg), ("own", feats, group.at[y]), ("vals", vals_h, vals),
-        ("ws", w_self, ws), ("wn", w_neigh, wn), ("mom", mom_h, mom), ("gmom", gmom_h, gmom), ("cot", cot_h, cot),
-    ]):
-        loads[name] = pltpu.make_async_copy(s, d, lsem.at[i])
-        loads[name].start()
-
     barrier = pltpu.get_barrier_semaphore()
 
     def greet(peer):
         pl.semaphore_signal(barrier, inc=1, device_id=peer, device_id_type=MESH)
 
-    def sig(d, _):
-        greet((((chip + d) % CHIPS) * 2 + core, y))
-        return 0
-
-    lax.fori_loop(1, CHIPS, sig, 0)
+    for dx, dz in sheet:
+        greet(device((x + dx) % XS, (z + dz) % ZS, y))
     greet(sibling)
     away = [(dx, dy) for dx, dy in plane if dy]
     for dx, dy in away:
         px, py = at_plane(dx, dy)
         greet(device(px, z, py))
 
+    loads = {}
+    for i, (name, s, d) in enumerate([
+        ("mir", mir_h, mir), ("cnt", cnt_h, cnt), ("pp", pp_h, pp), ("mas", mas_h, mas), ("pg", pg_h, pg), ("own", feats, group.at[y]), ("vals", vals_h, vals),
+        ("ws", w_self, ws), ("wn", w_neigh, wn), ("mom", mom_h, mom), ("gmom", gmom_h, gmom), ("cot", cot_h, cot),
+        ("dst", dst_h, dst), ("src", src_h, src), ("count", count_h, count),
+    ]):
+        loads[name] = pltpu.make_async_copy(s, d, lsem.at[i])
+        loads[name].start()
+
+    for name in ("mir", "cnt", "mas"):
+        loads[name].wait()
     nk = 4 * N_GRAPH
     cnt_row = jnp.concatenate([cnt[...]] * 4, axis=1)
     slot_row = lax.broadcasted_iota(jnp.int32, (1, nk), 1) // N_GRAPH
@@ -100,24 +110,20 @@
 
     pl.semaphore_wait(barrier, CHIPS + len(away))
 
-    ag = []
-    for d in range(1, YS):
+    ag = {}
+    for d in slabs:
         cp = pltpu.make_async_remote_copy(
             feats, group.at[y], ag_s.at[d - 1], ag_r.at[d - 1],
             device_id=(g, (y + d) % YS), device_id_type=MESH)
         cp.start()
-        ag.append(cp)
+        ag[d] = cp
 
     for t in range(2):
-
-        def send(d, _):
-            peer = (chip + d) % CHIPS
+        for dx, dz in sheet:
+            px, pz = (x + dx) % XS, (z + dz) % ZS
             pltpu.make_async_remote_copy(
-                msg.at[t, peer], inbox.at[t, chip, core], a2a_s.at[t], a2a_r.at[t],
-                device_id=(peer * 2 + core, y), device_id_type=MESH).start()
-            return 0
-
-        lax.fori_loop(1, CHIPS, send, 0)
+                msg.at[t, px * ZS + pz], inbox.at[t, chip, core], a2a_s.at[t], a2a_r.at[t],
+                device_id=device(px, pz, y), device_id_type=MESH).start()
 
     def forward(t):
         some = inbox.at[t, pl.ds(0, CHIPS - 1), 0]
@@ -138,6 +144,8 @@
         return jnp.concatenate(halves, axis=1).astype(BF)
 
     loads["vals"].wait()
+    for name in ("dst", "src", "count"):
+        loads[name].wait()
     n_live = count[0, 0]
     cells = []
     for b in range(32):
@@ -170,9 +178,9 @@
     loads["wn"].wait()
     pre = dot(own, ws[...])
     local = dot(a_hi[y], own) + dot(a_lo[y], own)
-    for d in range(1, YS):
+    for d in slabs[::-1]:
         t = (y + YS - d) % YS
-        ag[d - 1].wait_recv()
+        ag[d].wait_recv()
         tile = group[t]
         local = local + dot(a_hi[t], tile) + dot(a_lo[t], tile)
 
@@ -228,7 +236,7 @@
     outs[-1].start()
     gagg = (dot_nt(delta, wn[...]) + sg).astype(BF)
     rs = []
-    for d in range(1, YS):
+    for d in slabs:
         t = (y + d) % YS
         s_rs[d - 1] = (dot(at_hi[t], gagg) + dot(at_lo[t], gagg)).astype(BF)
         cp = pltpu.make_async_remote_copy(
@@ -246,7 +254,7 @@
 
     r_c[z] = total.astype(BF)
     hop = []
-    for d in range(1, ZS):
+    for d in line:
         cp = pltpu.make_async_remote_copy(
             r_c.at[z], r_c.at[z], w_s.at[15 + d], w_r.at[15 + d],
             device_id=device(x, (z + d) % ZS, y), device_id_type=MESH)
@@ -281,19 +289,14 @@
         cp.wait_recv()
     ops += hop
     last = pltpu.make_async_remote_copy(
-        wfin.at[core], wfin.at[core], w_s.at[38], w_r.at[38], device_id=sibling, device_id_type=MESH)
+        wfin.at[core], wg_o.at[core], w_s.at[38], w_r.at[38], device_id=sibling, device_id_type=MESH)
     last.start()
     ops.append(last)
+    outs.append(pltpu.make_async_copy(wfin.at[core], wg_o.at[core], osem.at[4]))
+    outs[-1].start()
     last.wait_recv()
-    scale = 1.0 / (N_GRAPH * YS * 256) ** 0.5
-    for i in range(2):
-        for h in range(2):
-            wg_v[i, :, h * 128 : (h + 1) * 128] = (
-                wfin[i, h * 16 : (h + 1) * 16].astype(F32).reshape(256, 128) * scale)
-    outs.append(pltpu.make_async_copy(wg_v, wg_o, osem.at[4]))
-    outs[-1].start()
-
-    for cp in ag + fw + rs + ops:
+
+    for cp in list(ag.values()) + fw + rs + ops:
         cp.wait_send()
     for t in range(2):
         some = msg.at[t, pl.ds(0, CHIPS - 1)]
@@ -303,14 +306,20 @@
 
 
 def hand_over(*refs):
-    results, outs, stage, sem = refs[:5], refs[5:10], refs[10:15], refs[15]
+    results, outs, stage, wide, sem = refs[:5], refs[5:10], refs[10:15], refs[15], refs[16]
     order = (4, 2, 3, 0, 1)
     pull = [pltpu.make_async_copy(results[i], stage[i], sem.at[i]) for i in range(5)]
-    push = [pltpu.make_async_copy(stage[i], outs[i], sem.at[5 + i]) for i in range(5)]
+    push = [pltpu.make_async_copy(wide if i == 4 else stage[i], outs[i], sem.at[5 + i]) for i in range(5)]
     for i in order:
         pull[i].start()
     for i in order:
         pull[i].wait()
+        if i == 4:
+            scale = 1.0 / (N_GRAPH * YS * 256) ** 0.5
+            for k in range(2):
+                for h in range(2):
+                    wide[k, :, h * 128 : (h + 1) * 128] = (
+                        stage[4][k, h * 16 : (h + 1) * 16].astype(F32).reshape(256, 128) * scale)
         push[i].start()
     for i in order:
         push[i].wait()
@@ -322,28 +331,27 @@
 ):
     sds = jax.ShapeDtypeStruct
     hbm = pl.BlockSpec(memory_space=pl.ANY)
-    vm = pl.BlockSpec(memory_space=pltpu.VMEM)
-    sm = pl.BlockSpec(memory_space=pltpu.SMEM)
-    V = pltpu.VMEM
+    V, S = pltpu.VMEM, pltpu.SMEM
     dma = pltpu.SemaphoreType.DMA
     mat = lambda dt: V((256, 256), dt)
     results = pl.pallas_call(
         kernel,
         out_shape=(
             sds((256, 256), BF), sds((256, 256), BF), sds((256, 256), F32), sds((256, 256), F32),
-            sds((2, 256, 256), F32),
+            sds((2, 32, 16, 128), BF),
         ),
-        in_specs=[hbm, hbm, hbm, hbm, sm, sm, sm, hbm, vm, vm, vm, hbm, hbm, hbm, hbm],
+        in_specs=[hbm] * 15,
         out_specs=[hbm] * 5,
         scratch_shapes=[
             V((YS, 256, 256), BF), mat(BF), mat(BF), V((32, 128, 128), BF), mat(BF), mat(BF), mat(F32), mat(BF), mat(F32),
+            V((4, N_GRAPH), I32), V((4, N_GRAPH), I32), V((1, N_GRAPH), I32), S((1, 32), I32), S((1, 32), I32), S((1, 1), I32),
             V((2, N_GRAPH * 8, 128), F32), V((2, CHIPS, 16, 128), BF), V((2, CHIPS, CORES, 16, 128), BF),
             V((YS, 256, 256), BF), V((YS, 256, 256), BF), V((YS, 256, 256), BF), V((YS, 256, 256), BF),
             mat(BF), mat(BF), mat(F32), mat(F32),
             V((32, 16, 128), BF), V((32, 16, 128), BF), V((32, 16, 128), BF), V((32, 16, 128), F32),
-            V((XS * YS - 1, 2, 16, 128), BF), V((ZS, 2, 16, 128), BF), V((2, 32, 16, 128), BF), V((2, 256, 256), F32),
+            V((XS * YS - 1, 2, 16, 128), BF), V((ZS, 2, 16, 128), BF), V((2, 32, 16, 128), BF),
             V((YS - 1, 256, 256), BF), V((YS - 1, 256, 256), BF),
-            dma((9,)), dma((5,)), dma((YS - 1,)), dma((YS - 1,)), dma((2,)), dma((2,)), dma((2,)), dma((2,)),
+            dma((15,)), dma((5,)), dma((YS - 1,)), dma((YS - 1,)), dma((2,)), dma((2,)), dma((2,)), dma((2,)),
             dma((YS - 1,)), dma((YS - 1,)), dma((39,)), dma((39,)),
         ],
         compiler_params=pltpu.CompilerParams(
@@ -355,10 +363,10 @@
     )
     hidden, fgrad, sp, sg, wg = pl.pallas_call(
         hand_over,
-        out_shape=tuple(sds(r.shape, r.dtype) for r in results),
+        out_shape=tuple(sds(r.shape, r.dtype) for r in results[:4]) + (sds((2, 256, 256), F32),),
         in_specs=[hbm] * 5,
         out_specs=[hbm] * 5,
-        scratch_shapes=[V(r.shape, r.dtype) for r in results] + [dma((10,))],
+        scratch_shapes=[V(r.shape, r.dtype) for r in results] + [V((2, 256, 256), F32), dma((10,))],
         compiler_params=pltpu.CompilerParams(vmem_limit_bytes=62 * 1024 * 1024),
     )(*results)
     return hidden[None, None], fgrad[None, None], sp[None, None], sg[None, None], wg

time: 45.8 us -> 43.5 us (0.950)
  Pallas kernels: 44.4 us -> 42.1 us
    pallas_call x1, Pallas kernels: 42.2 us -> 40 us  [shards(): pl.pallas_call(kernel, out_shape=(sds((256, 256), BF), sds((256, 256), BF...]
where the time goes in v3:
time: 43.5 us; the launch traced here: 43.4 us
  Pallas kernels  42.1 us (97%)
  between operations  1.29 us (3%)
    pallas_call x1, Pallas kernels, shards(): pl.pallas_call(kernel, out_shape=(sds((256, 256), BF), sds((256, 256), BF...  40 us
    pallas_call x1, Pallas kernels, shards(): pl.pallas_call(hand_over, out_shape=tuple((sds(r.shape, r.dtype) for r in...  2.12 us

profile of v3, /device:TPU:1, one launch (start us, length us, event | category | flops | bytes accessed | tf_op | source)
XLA Modules:
  0.0 43.4 jit_solution(18131918631569969460)
XLA Ops:
  1.3 40.0 %shard_map.182 = (bf16[256,256]{1,0:T(8,128)(2,1)}, bf16[256,256]{1,0:T(8,128)(2,1)}, f32[256,256]{1,0:T(8,128)}, f32[256,256]{1,0:T(8,128)}, bf16[2,32,16,128]{3,2,1,0:T(8,128)(2,1)}) custom-call(bf16[256,256]{1,0:T(8,128)(2,1)} %bitcast.23, bf16[256,256]{1,0:T(8,128)(2,1)} %w_self.1, bf16[256,256]{1,0:T(8,128)(2,1)} %w_neigh.1, ...), custom_call_target="tpu_custom_call" | custom-call | tf_op jit(solution)/shard_map/pallas_call | solution.py:337
  41.3 2.1 %shard_map.183 = (bf16[256,256]{1,0:T(8,128)(2,1)}, bf16[256,256]{1,0:T(8,128)(2,1)}, f32[256,256]{1,0:T(8,128)}, f32[256,256]{1,0:T(8,128)}, f32[2,256,256]{2,1,0:T(8,128)}) custom-call(bf16[256,256]{1,0:T(8,128)(2,1)} %get-tuple-element.15.refs_0_, bf16[256,256]{1,0:T(8,128)(2,1)} %get-tuple-element.16.refs_1_, f32[256,256]{1,0:T(8,128)} %get-tuple-element.17.refs_2_, ...), custom_call_target="tpu_custom_call" | custom-call | tf_op jit(solution)/shard_map/pallas_call | solution.py:364

commit v4 on v3

--- a/solution.py
+++ b/solution.py
@@ -178,13 +178,13 @@
     loads["wn"].wait()
     pre = dot(own, ws[...])
     local = dot(a_hi[y], own) + dot(a_lo[y], own)
+    fw = [forward(0)]
     for d in slabs[::-1]:
         t = (y + YS - d) % YS
         ag[d].wait_recv()
         tile = group[t]
         local = local + dot(a_hi[t], tile) + dot(a_lo[t], tile)
 
-    fw = [forward(0)]
     loads["mom"].wait()
     loads["cot"].wait()
     fw[0].wait_recv()

time: 43.5 us -> 42.2 us (0.970)
  Pallas kernels: 42.1 us -> 40.8 us
    pallas_call x1, Pallas kernels: 40 us -> 38.7 us  [shards(): pl.pallas_call(kernel, out_shape=(sds((256, 256), BF), sds((256, 256), BF...]
where the time goes in v4:
time: 42.2 us; the launch traced here: 42.1 us
  Pallas kernels  40.8 us (97%)
  between operations  1.29 us (3%)
    pallas_call x1, Pallas kernels, shards(): pl.pallas_call(kernel, out_shape=(sds((256, 256), BF), sds((256, 256), BF...  38.7 us
    pallas_call x1, Pallas kernels, shards(): pl.pallas_call(hand_over, out_shape=tuple((sds(r.shape, r.dtype) for r in...  2.12 us

profile of v4, /device:TPU:1, one launch (start us, length us, event | category | flops | bytes accessed | tf_op | source)
XLA Modules:
  0.0 42.1 jit_solution(7131638866475285454)
XLA Ops:
  1.3 38.7 %shard_map.182 = (bf16[256,256]{1,0:T(8,128)(2,1)}, bf16[256,256]{1,0:T(8,128)(2,1)}, f32[256,256]{1,0:T(8,128)}, f32[256,256]{1,0:T(8,128)}, bf16[2,32,16,128]{3,2,1,0:T(8,128)(2,1)}) custom-call(bf16[256,256]{1,0:T(8,128)(2,1)} %bitcast.23, bf16[256,256]{1,0:T(8,128)(2,1)} %w_self.1, bf16[256,256]{1,0:T(8,128)(2,1)} %w_neigh.1, ...), custom_call_target="tpu_custom_call" | custom-call | tf_op jit(solution)/shard_map/pallas_call | solution.py:337
  40.0 2.1 %shard_map.183 = (bf16[256,256]{1,0:T(8,128)(2,1)}, bf16[256,256]{1,0:T(8,128)(2,1)}, f32[256,256]{1,0:T(8,128)}, f32[256,256]{1,0:T(8,128)}, f32[2,256,256]{2,1,0:T(8,128)}) custom-call(bf16[256,256]{1,0:T(8,128)(2,1)} %get-tuple-element.15.refs_0_, bf16[256,256]{1,0:T(8,128)(2,1)} %get-tuple-element.16.refs_1_, f32[256,256]{1,0:T(8,128)} %get-tuple-element.17.refs_2_, ...), custom_call_target="tpu_custom_call" | custom-call | tf_op jit(solution)/shard_map/pallas_call | solution.py:364

commit v5 on v4

--- a/solution.py
+++ b/solution.py
@@ -31,12 +31,11 @@
 
 def kernel(
     feats, w_self, w_neigh, vals_h, dst_h, src_h, count_h, pp_h, mir_h, cnt_h, mas_h, mom_h, cot_h, pg_h, gmom_h,
-    hidden_o, fgrad_o, sp_o, sg_o, wg_o,
+    hidden_o, fgrad_o, sp_o, sg_o, wfin,
     group, ws, wn, vals, pp, pg, mom, cot, gmom, mir, mas, cnt, dst, src, count,
     msgf, msg, inbox, a_hi, a_lo, at_hi, at_lo,
-    hid_v, fg_v, sp_v, sg_v,
-    s_a, r_a, s_b, acc_a, r_b, r_c, wfin, s_rs, r_rs,
-    lsem, osem, ag_s, ag_r, a2a_s, a2a_r, fw_s, fw_r, rs_s, rs_r, w_s, w_r,
+    s_a, r_a, s_b, acc_a, r_b, r_c, s_rs, r_rs,
+    lsem, ag_s, ag_r, a2a_s, a2a_r, fw_s, fw_r, rs_s, rs_r, w_s, w_r,
 ):
     g = lax.axis_index("graph")
     y = lax.axis_index("slab")
@@ -222,18 +221,12 @@
         cp.start()
         hop.append(cp)
 
-    sp_v[...] = sp
-    outs = [pltpu.make_async_copy(sp_v, sp_o, osem.at[0])]
-    outs[-1].start()
-    hid_v[...] = jnp.maximum(pre, 0.0).astype(BF)
-    outs.append(pltpu.make_async_copy(hid_v, hidden_o, osem.at[1]))
-    outs[-1].start()
+    sp_o[...] = sp
+    hidden_o[...] = jnp.maximum(pre, 0.0).astype(BF)
     loads["gmom"].wait()
     fw[1].wait_recv()
     sg = SMOOTHING * gmom[...] + (1.0 - SMOOTHING) * dot(s_mir, received(1))
-    sg_v[...] = sg
-    outs.append(pltpu.make_async_copy(sg_v, sg_o, osem.at[2]))
-    outs[-1].start()
+    sg_o[...] = sg
     gagg = (dot_nt(delta, wn[...]) + sg).astype(BF)
     rs = []
     for d in slabs:
@@ -281,19 +274,15 @@
         cp.wait_recv()
     for d in range(1, YS):
         fg = fg + r_rs[d - 1].astype(F32)
-    fg_v[...] = fg.astype(BF)
-    outs.append(pltpu.make_async_copy(fg_v, fgrad_o, osem.at[3]))
-    outs[-1].start()
+    fgrad_o[...] = fg.astype(BF)
 
     for cp in hop:
         cp.wait_recv()
     ops += hop
     last = pltpu.make_async_remote_copy(
-        wfin.at[core], wg_o.at[core], w_s.at[38], w_r.at[38], device_id=sibling, device_id_type=MESH)
+        wfin.at[core], wfin.at[core], w_s.at[38], w_r.at[38], device_id=sibling, device_id_type=MESH)
     last.start()
     ops.append(last)
-    outs.append(pltpu.make_async_copy(wfin.at[core], wg_o.at[core], osem.at[4]))
-    outs[-1].start()
     last.wait_recv()
 
     for cp in list(ag.values()) + fw + rs + ops:
@@ -301,28 +290,21 @@
     for t in range(2):
         some = msg.at[t, pl.ds(0, CHIPS - 1)]
         pltpu.make_async_copy(some, some, a2a_s.at[t]).wait()
-    for cp in outs:
+
+
+def hand_over(*refs):
+    results, outs, wide, sem = refs[:5], refs[5:10], refs[10], refs[11]
+    push = [pltpu.make_async_copy(results[i] if i < 4 else wide, outs[i], sem.at[i]) for i in range(5)]
+    for i in (2, 3, 0, 1):
+        push[i].start()
+    scale = 1.0 / (N_GRAPH * YS * 256) ** 0.5
+    for k in range(2):
+        for h in range(2):
+            wide[k, :, h * 128 : (h + 1) * 128] = (
+                results[4][k, h * 16 : (h + 1) * 16].astype(F32).reshape(256, 128) * scale)
+    push[4].start()
+    for cp in push:
         cp.wait()
-
-
-def hand_over(*refs):
-    results, outs, stage, wide, sem = refs[:5], refs[5:10], refs[10:15], refs[15], refs[16]
-    order = (4, 2, 3, 0, 1)
-    pull = [pltpu.make_async_copy(results[i], stage[i], sem.at[i]) for i in range(5)]
-    push = [pltpu.make_async_copy(wide if i == 4 else stage[i], outs[i], sem.at[5 + i]) for i in range(5)]
-    for i in order:
-        pull[i].start()
-    for i in order:
-        pull[i].wait()
-        if i == 4:
-            scale = 1.0 / (N_GRAPH * YS * 256) ** 0.5
-            for k in range(2):
-                for h in range(2):
-                    wide[k, :, h * 128 : (h + 1) * 128] = (
-                        stage[4][k, h * 16 : (h + 1) * 16].astype(F32).reshape(256, 128) * scale)
-        push[i].start()
-    for i in order:
-        push[i].wait()
 
 
 def shards(
@@ -331,43 +313,42 @@
 ):
     sds = jax.ShapeDtypeStruct
     hbm = pl.BlockSpec(memory_space=pl.ANY)
+    vm = pl.BlockSpec(memory_space=pltpu.VMEM)
     V, S = pltpu.VMEM, pltpu.SMEM
     dma = pltpu.SemaphoreType.DMA
     mat = lambda dt: V((256, 256), dt)
     results = pl.pallas_call(
         kernel,
         out_shape=(
-            sds((256, 256), BF), sds((256, 256), BF), sds((256, 256), F32), sds((256, 256), F32),
-            sds((2, 32, 16, 128), BF),
+            mat(BF), mat(BF), mat(F32), mat(F32), V((2, 32, 16, 128), BF),
         ),
         in_specs=[hbm] * 15,
-        out_specs=[hbm] * 5,
+        out_specs=[vm] * 5,
         scratch_shapes=[
             V((YS, 256, 256), BF), mat(BF), mat(BF), V((32, 128, 128), BF), mat(BF), mat(BF), mat(F32), mat(BF), mat(F32),
             V((4, N_GRAPH), I32), V((4, N_GRAPH), I32), V((1, N_GRAPH), I32), S((1, 32), I32), S((1, 32), I32), S((1, 1), I32),
             V((2, N_GRAPH * 8, 128), F32), V((2, CHIPS, 16, 128), BF), V((2, CHIPS, CORES, 16, 128), BF),
             V((YS, 256, 256), BF), V((YS, 256, 256), BF), V((YS, 256, 256), BF), V((YS, 256, 256), BF),
-            mat(BF), mat(BF), mat(F32), mat(F32),
             V((32, 16, 128), BF), V((32, 16, 128), BF), V((32, 16, 128), BF), V((32, 16, 128), F32),
-            V((XS * YS - 1, 2, 16, 128), BF), V((ZS, 2, 16, 128), BF), V((2, 32, 16, 128), BF),
+            V((XS * YS - 1, 2, 16, 128), BF), V((ZS, 2, 16, 128), BF),
             V((YS - 1, 256, 256), BF), V((YS - 1, 256, 256), BF),
-            dma((15,)), dma((5,)), dma((YS - 1,)), dma((YS - 1,)), dma((2,)), dma((2,)), dma((2,)), dma((2,)),
+            dma((15,)), dma((YS - 1,)), dma((YS - 1,)), dma((2,)), dma((2,)), dma((2,)), dma((2,)),
             dma((YS - 1,)), dma((YS - 1,)), dma((39,)), dma((39,)),
         ],
         compiler_params=pltpu.CompilerParams(
-            collective_id=0, has_side_effects=True, vmem_limit_bytes=62 * 1024 * 1024),
-    )(
+            collective_id=0, has_side_effects=True, vmem_limit_bytes=24 * 1024 * 1024),
+    )(*[a if a.size == 1 else pltpu.with_memory_space_constraint(a, pltpu.HBM) for a in (
         feats[0, 0], w_self, w_neigh, block_vals[0, 0], block_dst[0], block_src[0], block_count,
         prev_partial[0, 0], jnp.swapaxes(mirror_rows[0, 0], 0, 1), send_count[0], jnp.swapaxes(master_rows[0, 0], 0, 1),
         momentum[0, 0], cotangent[0, 0], prev_grad[0, 0], grad_momentum[0, 0],
-    )
+    )])
     hidden, fgrad, sp, sg, wg = pl.pallas_call(
         hand_over,
         out_shape=tuple(sds(r.shape, r.dtype) for r in results[:4]) + (sds((2, 256, 256), F32),),
-        in_specs=[hbm] * 5,
+        in_specs=[vm] * 5,
         out_specs=[hbm] * 5,
-        scratch_shapes=[V(r.shape, r.dtype) for r in results] + [V((2, 256, 256), F32), dma((10,))],
-        compiler_params=pltpu.CompilerParams(vmem_limit_bytes=62 * 1024 * 1024),
+        scratch_shapes=[V((2, 256, 256), F32), dma((5,))],
+        compiler_params=pltpu.CompilerParams(vmem_limit_bytes=24 * 1024 * 1024),
     )(*results)
     return hidden[None, None], fgrad[None, None], sp[None, None], sg[None, None], wg
 

time: 42.2 us -> 41 us (0.972)
  Pallas kernels: 40.8 us -> 39.6 us
    pallas_call x1, Pallas kernels: 2.12 us -> 1.1 us  [shards(): pl.pallas_call(hand_over, out_shape=tuple((sds(r.shape, r.dtype) for r in...]
where the time goes in v5:
time: 41 us; the launch traced here: 40.9 us
  Pallas kernels  39.6 us (97%)
  between operations  1.29 us (3%)
    pallas_call x1, Pallas kernels, shards(): pl.pallas_call(kernel, out_shape=(mat(BF), mat(BF), mat(F32), mat(F32), V...  38.5 us
    pallas_call x1, Pallas kernels, shards(): pl.pallas_call(hand_over, out_shape=tuple((sds(r.shape, r.dtype) for r in...  1.1 us

profile of v5, /device:TPU:1, one launch (start us, length us, event | category | flops | bytes accessed | tf_op | source)
XLA Modules:
  0.0 40.9 jit_solution(10154424200111687196)
XLA Ops:
  1.3 38.5 %shard_map.182 = (bf16[256,256]{1,0:T(8,128)(2,1)S(1)}, bf16[256,256]{1,0:T(8,128)(2,1)S(1)}, f32[256,256]{1,0:T(8,128)S(1)}, f32[256,256]{1,0:T(8,128)S(1)}, bf16[2,32,16,128]{3,2,1,0:T(8,128)(2,1)S(1)}) custom-call(bf16[256,256]{1,0:T(8,128)(2,1)} %bitcast.23, bf16[256,256]{1,0:T(8,128)(2,1)} %w_self.1, bf16[256,256]{1,0:T(8,128)(2,1)} %w_neigh.1, ...), custom_call_target="tpu_custom_call" | custom-call | tf_op jit(solution)/shard_map/pallas_call | solution.py:320
  39.8 1.1 %shard_map.183 = (bf16[256,256]{1,0:T(8,128)(2,1)}, bf16[256,256]{1,0:T(8,128)(2,1)}, f32[256,256]{1,0:T(8,128)}, f32[256,256]{1,0:T(8,128)}, f32[2,256,256]{2,1,0:T(8,128)}) custom-call(bf16[256,256]{1,0:T(8,128)(2,1)S(1)} %get-tuple-element.15.refs_0_, bf16[256,256]{1,0:T(8,128)(2,1)S(1)} %get-tuple-element.16.refs_1_, ...), custom_call_target="tpu_custom_call" | custom-call | tf_op jit(solution)/shard_map/pallas_call | solution.py:345

commit v6 on v5

--- a/solution.py
+++ b/solution.py
@@ -109,10 +109,11 @@
 
     pl.semaphore_wait(barrier, CHIPS + len(away))
 
+    loads["own"].wait()
     ag = {}
     for d in slabs:
         cp = pltpu.make_async_remote_copy(
-            feats, group.at[y], ag_s.at[d - 1], ag_r.at[d - 1],
+            group.at[y], group.at[y], ag_s.at[d - 1], ag_r.at[d - 1],
             device_id=(g, (y + d) % YS), device_id_type=MESH)
         cp.start()
         ag[d] = cp
@@ -171,7 +172,6 @@
     for t in range(YS):
         at_hi[t] = a_hi[t].T
         at_lo[t] = a_lo[t].T
-    loads["own"].wait()
     own = group[y]
     loads["ws"].wait()
     loads["wn"].wait()
@@ -195,21 +195,22 @@
     def tiles(m, h):
         return m[:, h * 128 : (h + 1) * 128].reshape(16, 16, 128)
 
-    given = dot_tn(jnp.where(core == 0, agg, own), delta)
+    ops = []
+    lhs = jnp.where(core == 0, agg, own)
     for h in range(2):
-        s_a[h * 16 : (h + 1) * 16] = tiles(given, h).astype(BF)
-    cp_a = pltpu.make_async_remote_copy(
-        s_a, r_a, w_s.at[0], w_r.at[0], device_id=sibling, device_id_type=MESH)
-    cp_a.start()
-    fw.append(forward(1))
+        part = pl.ds(h * 16, 16)
+        s_a[part] = dot_tn(lhs, delta[:, h * 128 : (h + 1) * 128]).reshape(16, 16, 128).astype(BF)
+        cp = pltpu.make_async_remote_copy(
+            s_a.at[part], r_a.at[part], w_s.at[39 * h], w_r.at[39 * h], device_id=sibling, device_id_type=MESH)
+        cp.start()
+        ops.append(cp)
     kept = dot_tn(jnp.where(core == 0, own, agg), delta)
-    cp_a.wait_recv()
     for h in range(2):
+        ops[h].wait_recv()
         part = slice(h * 16, (h + 1) * 16)
         total = tiles(kept, h) + r_a[part].astype(F32)
         acc_a[part] = total
         s_b[part] = total.astype(BF)
-    ops = [cp_a]
 
     place = x * YS + y
     hop = []
@@ -221,6 +222,7 @@
         cp.start()
         hop.append(cp)
 
+    fw.append(forward(1))
     sp_o[...] = sp
     hidden_o[...] = jnp.maximum(pre, 0.0).astype(BF)
     loads["gmom"].wait()
@@ -235,7 +237,6 @@
         cp = pltpu.make_async_remote_copy(
             s_rs.at[d - 1], r_rs.at[d - 1], rs_s.at[d - 1], rs_r.at[d - 1],
             device_id=(g, t), device_id_type=MESH)
-        cp.start()
         rs.append(cp)
 
     for cp in hop:
@@ -253,6 +254,8 @@
             device_id=device(x, (z + d) % ZS, y), device_id_type=MESH)
         cp.start()
         hop.append(cp)
+    for cp in rs:
+        cp.start()
     fg = dot_nt(delta, ws[...]) + dot(at_hi[y], gagg) + dot(at_lo[y], gagg)
     for cp in hop:
         cp.wait_recv()
@@ -333,7 +336,7 @@
             V((XS * YS - 1, 2, 16, 128), BF), V((ZS, 2, 16, 128), BF),
             V((YS - 1, 256, 256), BF), V((YS - 1, 256, 256), BF),
             dma((15,)), dma((YS - 1,)), dma((YS - 1,)), dma((2,)), dma((2,)), dma((2,)), dma((2,)),
-            dma((YS - 1,)), dma((YS - 1,)), dma((39,)), dma((39,)),
+            dma((YS - 1,)), dma((YS - 1,)), dma((40,)), dma((40,)),
         ],
         compiler_params=pltpu.CompilerParams(
             collective_id=0, has_side_effects=True, vmem_limit_bytes=24 * 1024 * 1024),

time: 41 us -> 40.7 us (level)
  no operation moved by 1% of the time
where the time goes in v6:
time: 40.7 us; the launch traced here: 40.6 us
  Pallas kernels  39.3 us (97%)
  between operations  1.29 us (3%)
    pallas_call x1, Pallas kernels, shards(): pl.pallas_call(kernel, out_shape=(mat(BF), mat(BF), mat(F32), mat(F32), V...  38.2 us
    pallas_call x1, Pallas kernels, shards(): pl.pallas_call(hand_over, out_shape=tuple((sds(r.shape, r.dtype) for r in...  1.1 us

profile of v6, /device:TPU:1, one launch (start us, length us, event | category | flops | bytes accessed | tf_op | source)
XLA Modules:
  0.0 40.6 jit_solution(11926407204713253176)
XLA Ops:
  1.3 38.2 %shard_map.182 = (bf16[256,256]{1,0:T(8,128)(2,1)S(1)}, bf16[256,256]{1,0:T(8,128)(2,1)S(1)}, f32[256,256]{1,0:T(8,128)S(1)}, f32[256,256]{1,0:T(8,128)S(1)}, bf16[2,32,16,128]{3,2,1,0:T(8,128)(2,1)S(1)}) custom-call(bf16[256,256]{1,0:T(8,128)(2,1)} %bitcast.23, bf16[256,256]{1,0:T(8,128)(2,1)} %w_self.1, bf16[256,256]{1,0:T(8,128)(2,1)} %w_neigh.1, ...), custom_call_target="tpu_custom_call" | custom-call | tf_op jit(solution)/shard_map/pallas_call | solution.py:323
  39.5 1.1 %shard_map.183 = (bf16[256,256]{1,0:T(8,128)(2,1)}, bf16[256,256]{1,0:T(8,128)(2,1)}, f32[256,256]{1,0:T(8,128)}, f32[256,256]{1,0:T(8,128)}, f32[2,256,256]{2,1,0:T(8,128)}) custom-call(bf16[256,256]{1,0:T(8,128)(2,1)S(1)} %get-tuple-element.15.refs_0_, bf16[256,256]{1,0:T(8,128)(2,1)S(1)} %get-tuple-element.16.refs_1_, ...), custom_call_target="tpu_custom_call" | custom-call | tf_op jit(solution)/shard_map/pallas_call | solution.py:348
